TPU v7x, 32 devices: a whole 2x2x4 slice. The times are simulated.
32 devices in a mesh: experts: 8 (over z, y), context: 4 (over x, core).
Axes of the slice: x: 2, y: 2, z: 4, core: 2. Of those that a mesh axis runs over, the one named last changes fastest.
Arguments:
- block_input: bfloat16 [8, 512, 768], P('experts', 'context'), may hold values from -6 to 6
- first_gain: float32 [768], replicated, may hold values from 0.5 to 1.5
- second_gain: float32 [768], replicated, may hold values from 0.5 to 1.5
- qkv_weight: bfloat16 [768, 2304], replicated, may hold values from -0.21875 to 0.21875
- out_weight: bfloat16 [768, 768], replicated, may hold values from -0.21875 to 0.21875
- rel_table: float32 [32, 12], replicated, may hold values from -2 to 2
- bucket_ids: int32 [512, 512], P('context'), may hold values from 0 to 31
- expert_route: int32 [8, 512], P('experts', 'context'), may hold values from 0 to 15, as said below
- expert_slot: int32 [8, 512], P('experts', 'context'), may hold values from 0 to 9, as said below
- gate_value: float32 [8, 512], P('experts', 'context'), may hold values from 0.5 to 1.5
- expert_in: bfloat16 [16, 768, 3072], P('experts', None, 'context'), may hold values from -0.21875 to 0.21875
- expert_down: bfloat16 [16, 3072, 768], P('experts', 'context'), may hold values from -0.15625 to 0.15625
- upstream: bfloat16 [8, 512, 768], P('experts', 'context'), may hold values from -6 to 6
Outputs:
- block_output: bfloat16 [8, 512, 768], P('experts', 'context')
- input_grad: float32 [8, 512, 768], P('experts', 'context')
- qkv_grad: float32 [768, 2304], P('experts')
- proj_grad: float32 [768, 768], P('experts')
- first_grad: float32 [768], P('experts')
- second_grad: float32 [768], P('experts')
- table_grad: float32 [32, 12], P('experts')
- inner_grad: float32 [16, 768, 3072], P('experts', None, 'context')
- down_grad: float32 [16, 3072, 768], P('experts', 'context')
Inputs may be any that keep to these rules, and one draw needn't show every extreme that they name: `expert_route`: within each aligned block of 128 consecutive tokens of a sequence no expert is named by more than 10 tokens; one expert, the same in every block, is named by exactly 10 tokens in every block, and so is a second one drawn for each block (in some blocks the two are the same expert); the other tokens of a block spread over the remaining slots. Within each aligned block of 128 tokens the pairs of expert_route and expert_slot are distinct.
All inputs are finite; a program needn't handle non-finite values.
Results may differ from a plain program's by a relative error of at most 0.033.
Values may be sent and summed in bfloat16 or wider, within the bound.
A program may use at most 192 MiB of HBM per device.

v0:
```python
import math

import jax
import jax.numpy as jnp
from jax import lax
from jax.sharding import PartitionSpec as P

norm_eps = 1e-06
floor_value = -1e30


def rms_scale(values, gain):
    factor = lax.rsqrt(jnp.mean(values * values, axis=-1, keepdims=True) + norm_eps)
    return values * factor * gain


def block_width(total_rows, local_rows):
    step_rows = local_rows
    while total_rows % (step_rows * 2) == 0 and step_rows * 2 <= 512:
        step_rows = step_rows * 2
    return step_rows


def forward_piece(state, piece, queries, bucket_rows, table_heads):
    head_count = table_heads.shape[0]
    local_rows, model_width = queries.shape
    head_size = model_width // head_count
    total_rows = piece.shape[0]
    step_rows = block_width(total_rows, local_rows)
    score_scale = 1.0 / math.sqrt(head_size)
    q_heads = queries.reshape(local_rows, head_count, head_size)

    def forward_one_block(index, carry):
        running_max, running_sum, accum = carry
        offset = index * step_rows
        key_block = lax.dynamic_slice_in_dim(piece, offset, step_rows, 0)
        columns = lax.dynamic_slice_in_dim(bucket_rows, offset, step_rows, 1)
        k_heads = key_block[:, :model_width].reshape(step_rows, head_count, head_size)
        v_heads = (
            key_block[:, model_width:].reshape(step_rows, head_count, head_size).astype(jnp.float32)
        )
        dots = jnp.einsum("qhd,khd->hqk", q_heads, k_heads, preferred_element_type=jnp.float32)
        scores = dots * score_scale + jnp.take(table_heads, columns, axis=1)
        new_max = jnp.maximum(running_max, jnp.max(scores, axis=-1))
        shrink = jnp.exp(running_max - new_max)
        expons = jnp.exp(scores - new_max[:, :, None])
        running_sum = running_sum * shrink + jnp.sum(expons, axis=-1)
        product = jnp.einsum("hqk,khd->hqd", expons, v_heads, precision=lax.Precision.HIGHEST)
        accum = accum * shrink[:, :, None] + product
        return (new_max, running_sum, accum)

    return lax.fori_loop(0, total_rows // step_rows, forward_one_block, state)


def backward_piece(state, piece, queries, d_att, log_total, delta, bucket_rows, table_heads):
    head_count, bucket_count = table_heads.shape
    local_rows, model_width = queries.shape
    head_size = model_width // head_count
    total_rows = piece.shape[0]
    step_rows = block_width(total_rows, local_rows)
    score_scale = 1.0 / math.sqrt(head_size)
    q_heads = queries.reshape(local_rows, head_count, head_size)
    grad_heads = d_att.reshape(local_rows, head_count, head_size)
    bucket_range = jnp.arange(bucket_count, dtype=jnp.int32)

    def backward_one_block(index, carry):
        d_query, table_sum, d_key_value = carry
        offset = index * step_rows
        key_block = lax.dynamic_slice_in_dim(piece, offset, step_rows, 0)
        columns = lax.dynamic_slice_in_dim(bucket_rows, offset, step_rows, 1)
        k_heads = key_block[:, :model_width].reshape(step_rows, head_count, head_size)
        v_heads = key_block[:, model_width:].reshape(step_rows, head_count, head_size)
        dots = jnp.einsum("qhd,khd->hqk", q_heads, k_heads, preferred_element_type=jnp.float32)
        scores = dots * score_scale + jnp.take(table_heads, columns, axis=1)
        probs_wide = jnp.exp(scores - log_total[:, :, None])
        weights = probs_wide.astype(jnp.bfloat16)
        d_probs = jnp.einsum(
            "qhd,khd->hqk", grad_heads, v_heads, preferred_element_type=jnp.float32
        )
        d_scores = probs_wide * (d_probs - delta[:, :, None])
        d_scores_b = d_scores.astype(jnp.bfloat16)
        d_query = (
            d_query
            + jnp.einsum("hqk,khd->qhd", d_scores_b, k_heads, preferred_element_type=jnp.float32)
            * score_scale
        )
        d_keys = (
            jnp.einsum("hqk,qhd->khd", d_scores_b, q_heads, preferred_element_type=jnp.float32)
            * score_scale
        )
        d_values = jnp.einsum(
            "hqk,qhd->khd", weights, grad_heads, preferred_element_type=jnp.float32
        )
        one_hot = (columns[:, :, None] == bucket_range).astype(jnp.float32)
        table_sum = table_sum + jnp.einsum(
            "hqk,qkb->bh", d_scores, one_hot, precision=lax.Precision.HIGHEST
        )
        current = lax.dynamic_slice_in_dim(d_key_value, offset, step_rows, 0)
        update = jnp.concatenate(
            [d_keys.reshape(step_rows, model_width), d_values.reshape(step_rows, model_width)],
            axis=1,
        )
        d_key_value = lax.dynamic_update_slice_in_dim(d_key_value, current + update, offset, 0)
        return (d_query, table_sum, d_key_value)

    return lax.fori_loop(0, total_rows // step_rows, backward_one_block, state)


def body(
    block_input,
    first_gain,
    second_gain,
    qkv_weight,
    out_weight,
    rel_table,
    bucket_ids,
    expert_route,
    expert_slot,
    gate_value,
    expert_in,
    expert_down,
    upstream,
):
    features = block_input[0].astype(jnp.float32)
    local_rows, model_width = features.shape
    head_count = rel_table.shape[1]
    head_size = model_width // head_count
    seq_tokens = bucket_ids.shape[1]
    table_heads = rel_table.T
    normed = rms_scale(features, first_gain).astype(jnp.bfloat16)
    qkv_local = jnp.dot(normed, qkv_weight, preferred_element_type=jnp.float32).astype(jnp.bfloat16)
    queries = qkv_local[:, :model_width]
    key_value = qkv_local[:, model_width:]
    start_state = (
        jnp.full((head_count, local_rows), floor_value, jnp.float32),
        jnp.zeros((head_count, local_rows), jnp.float32),
        jnp.zeros((head_count, local_rows, head_size), jnp.float32),
    )
    running_max, running_sum, accum = forward_piece(
        start_state,
        lax.all_gather(key_value, "context", axis=0, tiled=True),
        queries,
        bucket_ids,
        table_heads,
    )
    log_total = running_max + jnp.log(running_sum)
    attended = (
        (accum / running_sum[:, :, None])
        .transpose(1, 0, 2)
        .reshape(local_rows, model_width)
        .astype(jnp.bfloat16)
    )
    middle = features + jnp.dot(attended, out_weight, preferred_element_type=jnp.float32)
    second_normed = rms_scale(middle, second_gain)
    experts_local = expert_in.shape[0]
    expert_ranks = lax.axis_size("experts")
    experts_total = experts_local * expert_ranks
    capacity = max(4, 4 * local_rows // (3 * experts_total))
    routes = expert_route[0]
    slot_ids = expert_slot[0]
    gates = gate_value[0][:, None]

    def to_buckets(token_rows):
        empty = jnp.zeros((experts_total, capacity, model_width), token_rows.dtype)
        return (
            empty.at[routes, slot_ids]
            .set(token_rows)
            .reshape(expert_ranks, experts_local, capacity, model_width)
        )

    def from_buckets(arrived_rows):
        return arrived_rows.reshape(experts_total, capacity, model_width)[routes, slot_ids]

    arrived = lax.all_to_all(
        to_buckets(second_normed), "experts", split_axis=0, concat_axis=0, tiled=True
    )
    gathered = lax.all_gather(arrived, "context", axis=0, tiled=True)
    weight_wide = expert_in.astype(jnp.float32)
    pre_act = jnp.einsum("bxcd,xdf->bxcf", gathered, weight_wide, precision=lax.Precision.HIGHEST)
    hidden = jnp.maximum(pre_act, 0.0).astype(jnp.bfloat16)
    part_rows = hidden
    summed = lax.psum_scatter(
        jnp.einsum(
            "bxcf,xfd->bxcd", part_rows, expert_down, preferred_element_type=jnp.float32
        ).astype(jnp.bfloat16),
        "context",
        scatter_dimension=0,
        tiled=True,
    )
    returned = lax.all_to_all(summed, "experts", split_axis=0, concat_axis=0, tiled=True)
    picked = from_buckets(returned).astype(jnp.float32)
    block_output = (middle + gates * picked).astype(jnp.bfloat16)[None]
    grad_top = upstream[0].astype(jnp.float32)
    sent_back = lax.all_to_all(
        to_buckets((gates * grad_top).astype(jnp.bfloat16)),
        "experts",
        split_axis=0,
        concat_axis=0,
        tiled=True,
    )
    grad_rows = lax.all_gather(sent_back, "context", axis=0, tiled=True)
    down_grad = jnp.einsum("bxcf,bxcd->xfd", hidden, grad_rows, preferred_element_type=jnp.float32)
    hidden_grad = jnp.einsum(
        "bxcd,xfd->bxcf", grad_rows, expert_down, preferred_element_type=jnp.float32
    )
    pre_grad = jnp.where(pre_act > 0.0, hidden_grad, 0.0).astype(jnp.bfloat16)
    inner_grad = jnp.einsum(
        "bxcd,bxcf->xdf", gathered, pre_grad.astype(jnp.float32), precision=lax.Precision.HIGHEST
    )
    part_rows = pre_grad
    summed_back = lax.psum_scatter(
        jnp.einsum("bxcf,xdf->bxcd", part_rows, expert_in, preferred_element_type=jnp.float32),
        "context",
        scatter_dimension=0,
        tiled=True,
    )
    returned_back = lax.all_to_all(
        summed_back.astype(jnp.bfloat16), "experts", split_axis=0, concat_axis=0, tiled=True
    )
    d_second = from_buckets(returned_back).astype(jnp.float32)
    _, second_pull = jax.vjp(rms_scale, middle, second_gain)
    d_middle_norm, second_part = second_pull(d_second)
    d_middle = grad_top + d_middle_norm
    d_middle_b = d_middle.astype(jnp.bfloat16)
    proj_part = jnp.einsum("td,te->de", attended, d_middle_b, preferred_element_type=jnp.float32)
    d_att = jnp.einsum(
        "te,de->td", d_middle_b, out_weight, preferred_element_type=jnp.float32
    ).astype(jnp.bfloat16)
    delta = jnp.sum(
        (d_att.astype(jnp.float32) * attended.astype(jnp.float32)).reshape(
            local_rows, head_count, head_size
        ),
        axis=-1,
    ).T
    back_state = (
        jnp.zeros((local_rows, head_count, head_size), jnp.float32),
        jnp.zeros(rel_table.shape, jnp.float32),
        jnp.zeros((seq_tokens, 2 * model_width), jnp.float32),
    )
    d_query, table_part, d_key_value = backward_piece(
        back_state,
        lax.all_gather(key_value, "context", axis=0, tiled=True),
        queries,
        d_att,
        log_total,
        delta,
        bucket_ids,
        table_heads,
    )
    own_grads = lax.psum_scatter(
        d_key_value.astype(jnp.bfloat16), "context", scatter_dimension=0, tiled=True
    ).astype(jnp.float32)
    d_qkv = jnp.concatenate([d_query.reshape(local_rows, model_width), own_grads], axis=1).astype(
        jnp.bfloat16
    )
    qkv_part = jnp.einsum("td,te->de", normed, d_qkv, preferred_element_type=jnp.float32)
    d_first = jnp.einsum("te,de->td", d_qkv, qkv_weight, preferred_element_type=jnp.float32)
    _, first_pull = jax.vjp(rms_scale, features, first_gain)
    d_input_norm, first_part = first_pull(d_first)
    input_grad = (d_middle + d_input_norm)[None]
    qkv_shard, proj_shard, first_shard, second_shard, table_shard = (
        lax.psum_scatter(
            qkv_part.astype(jnp.bfloat16), "experts", scatter_dimension=0, tiled=True
        ).astype(jnp.float32),
        lax.psum_scatter(
            proj_part.astype(jnp.bfloat16), "experts", scatter_dimension=0, tiled=True
        ).astype(jnp.float32),
        lax.psum_scatter(
            first_part.astype(jnp.bfloat16), "experts", scatter_dimension=0, tiled=True
        ).astype(jnp.float32),
        lax.psum_scatter(
            second_part.astype(jnp.bfloat16), "experts", scatter_dimension=0, tiled=True
        ).astype(jnp.float32),
        lax.psum_scatter(
            table_part.astype(jnp.bfloat16), "experts", scatter_dimension=0, tiled=True
        ).astype(jnp.float32),
    )
    qkv_grad, proj_grad, first_grad, second_grad, table_grad = (
        lax.psum(qkv_shard.astype(jnp.bfloat16), "context").astype(jnp.float32),
        lax.psum(proj_shard.astype(jnp.bfloat16), "context").astype(jnp.float32),
        lax.psum(first_shard.astype(jnp.bfloat16), "context").astype(jnp.float32),
        lax.psum(second_shard.astype(jnp.bfloat16), "context").astype(jnp.float32),
        lax.psum(table_shard.astype(jnp.bfloat16), "context").astype(jnp.float32),
    )
    return (
        block_output,
        input_grad,
        qkv_grad,
        proj_grad,
        first_grad,
        second_grad,
        table_grad,
        inner_grad,
        down_grad,
    )


def solution(mesh):
    placed = (
        P("experts", "context", None),
        P(),
        P(),
        P(),
        P(),
        P(),
        P("context", None),
        P("experts", "context"),
        P("experts", "context"),
        P("experts", "context"),
        P("experts", None, "context"),
        P("experts", "context", None),
        P("experts", "context", None),
    )
    return jax.shard_map(
        body,
        mesh=mesh,
        in_specs=placed,
        out_specs=(
            P("experts", "context", None),
            P("experts", "context", None),
            P("experts", None),
            P("experts", None),
            P("experts"),
            P("experts"),
            P("experts", None),
            P("experts", None, "context"),
            P("experts", "context", None),
        ),
        check_vma=False,
    )
```

profile of v0, /device:TPU:0, one launch (start us, length us, event | category | flops | bytes accessed | tf_op | source)
XLA Modules:
  0.0 730.5 jit_solution(279459442171392936)
XLA Ops:
  22.1 236.7 %gather_fusion.2 = f32[65536,12]{1,0:T(8,128)} fusion(f32[12,32]{0,1:T(8,128)S(1)} %bitcast.150, s32[65536]{0:T(1024)} %broadcast_clamp_fusion), kind=kCustom, calls=%fused_computation.clone | custom fusion | bytes 6553600 | tf_op jit(solution)/shard_map/while/body/eval_jaxpr/jit(_take)/gather | solution.py:43
  258.8 20.7 %copy.89 = f32[128,512,12]{1,0,2:T(8,128)} copy(f32[128,512,12]{2,1,0:T(8,128)} %bitcast.151) | data formatting | bytes 6291456 | tf_op jit(solution)/shard_map/while/body/eval_jaxpr/jit(_take)/gather | solution.py:43
  281.2 2.6 fusion.76
  283.9 2.3 copy.68
  286.2 3.1 fusion.77
  293.1 2.3 copy.71
  295.4 4.5 fusion.38
  302.8 18.1 %scatter_fusion = f32[16,10,768]{2,0,1:T(8,128)} fusion(f32[16,10,768]{2,0,1:T(8,128)} %broadcast_in_dim.37, s32[128]{0:T(128)S(1)} %get-tuple-element.88, f32[128,768]{1,0:T(8,128)} %multiply_multiply_fusion), kind=kCustom, calls=%fused_computation.3 | custom fusion | bytes 1180672 | tf_op jit(solution)/shard_map/scatter | solution.py:167
  320.9 2.1 reshape.198
  324.1 20.9 %all_to_all.20 = f32[8,2,10,768]{3,1,2,0:T(2,128)S(1)} all-to-all(f32[8,2,10,768]{3,1,2,0:T(2,128)S(1)} %copy.72), channel_id=1, replica_groups=mesh['experts'=8,'context'=4] {'experts'}, dimensions={0} | all-to-all | bytes 983040 | tf_op jit(solution)/shard_map/all_to_all | solution.py:174
  346.1 20.8 %all-gather.5.cloned.1.call-done = f32[32,2,10,768]{3,0,2,1:T(8,128)} async-done(((f32[8,2,10,768]{3,0,2,1:T(8,128)}), f32[32,2,10,768]{3,0,2,1:T(8,128)}) %all-gather.5.cloned.1.call-update) | async-done | bytes 1966096 | tf_op jit(solution)/shard_map/all_gather | solution.py:177
  366.9 4.9 fusion.7
  374.9 2.6 reshape.252
  380.0 18.1 %scatter_fusion.1 = bf16[16,10,768]{2,0,1:T(8,128)(2,1)} fusion(bf16[16,10,768]{2,0,1:T(8,128)(2,1)} %broadcast_in_dim.39, s32[128]{0:T(128)S(1)} %get-tuple-element.88, bf16[128,768]{1,0:T(8,128)(2,1)} %fusion.52), kind=kCustom, calls=%fused_computation.4 | custom fusion | bytes 590848 | tf_op jit(solution)/shard_map/scatter | solution.py:167
  401.0 14.5 %all_to_all.21 = bf16[8,2,10,768]{3,1,2,0:T(2,128)(2,1)S(1)} all-to-all(bf16[8,2,10,768]{3,1,2,0:T(2,128)(2,1)S(1)} %copy.76), channel_id=1, replica_groups=mesh['experts'=8,'context'=4] {'experts'}, dimensions={0} | all-to-all | bytes 491520 | tf_op jit(solution)/shard_map/all_to_all | solution.py:194
  415.5 8.6 %all_gather.12 = bf16[32,2,10,768]{3,0,2,1:T(8,128)(2,1)S(1)} all-gather(bf16[8,2,10,768]{3,0,2,1:T(8,128)(2,1)S(1)} %copy.77), channel_id=1, replica_groups=mesh['experts'=8,'context'=4] {'context'}, dimensions={0}, use_global_device_ids=true | all-gather | bytes 1228800 | tf_op jit(solution)/shard_map/all_gather | solution.py:201
  424.1 3.0 fusion.28
  428.2 2.2 fusion.13
  430.5 1.8 copy.74
  432.3 4.2 all-to-all-start.1
  436.5 23.8 %reduce-scatter.10.cloned.1.call-done = f32[8,2,10,768]{3,0,2,1:T(8,128)} async-done(((f32[32,2,10,768]{3,0,2,1:T(8,128)}), f32[8,2,10,768]{3,0,2,1:T(8,128)}) %reduce-scatter.10.cloned.1.call-update) | async-done | bytes 491536 | tf_op jit(solution)/shard_map/reduce_scatter | solution.py:211
  462.2 5.5 all-to-all-start.3
  469.7 1.8 copy.75
  473.3 3.1 gather_fusion
  476.5 1.8 copy.79
  480.1 3.1 gather_fusion.1
  483.2 1.9 fusion.51
  485.7 2.1 convert_add_fusion
  488.5 2.3 convert_multiply_fusion.7
  490.8 1.9 copy.82
  495.5 2.9 fusion.25
  503.2 2.6 copy.92
  505.9 2.6 convolution_convert_fusion.2
  508.5 3.5 fusion.37
  512.0 22.2 %reduce-scatter.18.cloned.1.call-done = bf16[128,1536]{1,0:T(8,128)(2,1)} async-done(((bf16[512,1536]{1,0:T(8,128)(2,1)}), bf16[128,1536]{1,0:T(8,128)(2,1)}) %reduce-scatter.18.cloned.1.call-update) | async-done | bytes 393232
  534.2 1.9 copy.93
  536.2 4.1 convolution_convert_fusion
  544.3 5.6 convolution_bitcast_fusion
  549.9 5.8 convolution_bitcast_fusion.1
  555.7 5.1 copy.84
  560.8 6.3 fusion.40
  567.2 2.6 fusion.49
  569.8 37.3 %all-reduce.3 = (bf16[768]{0:T(1024)(128)(2,1)}, bf16[768]{0:T(1024)(128)(2,1)}, bf16[32,12]{1,0:T(8,128)(2,1)}) all-reduce(bf16[768]{0:T(1024)(128)(2,1)} %get-tuple-element.65, bf16[768]{0:T(1024)(128)(2,1)S(1)} %copy-done.29, bf16[32,12]{1,0:T(8,128)(2,1)S(1)} %fusion.40), channel_id=7, replica_groups=mesh['experts'=8,'context'=4] {'experts'}, use_global_device_ids=true, to_apply=%region_17.19.clone | all-reduce | flops 1920 | bytes 7680
  607.8 76.5 %reduce-scatter.12.cloned.1.call-done = bf16[96,2304]{1,0:T(8,128)(2,1)} async-done(((bf16[768,2304]{1,0:T(8,128)(2,1)}), bf16[96,2304]{1,0:T(8,128)(2,1)}) %reduce-scatter.12.cloned.1.call-update) | async-done | bytes 442384 | tf_op jit(solution)/shard_map/reduce_scatter | solution.py:262
  687.5 6.9 all-reduce.4
  697.3 2.1 fusion.54
  699.4 20.7 %all-reduce.8.cloned.1.call-done = (bf16[96,2304]{1,0:T(8,128)(2,1)}, bf16[96,768]{1,0:T(8,128)(2,1)}) async-done(((bf16[96,2304]{1,0:T(8,128)(2,1)}, bf16[96,768]{1,0:T(8,128)(2,1)}), (bf16[96,2304]{1,0:T(8,128)(2,1)}, bf16[96,768]{1,0:T(8,128)(2,1)})) %all-reduce.8.cloned.1.call-update) | async-done | bytes 589840 | tf_op jit(solution)/shard_map/psum | solution.py:279
  720.1 2.0 convert_element_type.152
  (149 shorter events, 62.8 us)
Async XLA Ops:
  7.2 2.4 copy-start
  7.2 274.1 %all-gather.3.cloned.1.call-start = ((), (), s32[]{:S(2)}) async-start(), calls=%async_computation.9 | async-start | bytes 1966080 | tf_op jit(solution)/shard_map/all_gather | solution.py:141
  8.4 0.6 copy-start.34
  11.2 0.8 copy-start.18
  12.8 354.1 %all-gather.5.cloned.1.call-start = ((), (), s32[]{:S(2)}) async-start(), calls=%async_computation.10 | async-start | bytes 2457600 | tf_op jit(solution)/shard_map/all_gather | solution.py:177
  258.8 20.7 %copy-start.36 = (s32[1,128]{1,0:T(1,128)S(1)}, s32[1,128]{1,0:T(1,128)}, u32[]{:S(2)}) copy-start(s32[1,128]{1,0:T(1,128)} %param.22) | copy-start | bytes 1540
  258.8 20.7 %copy-start.37 = (s32[1,128]{1,0:T(1,128)S(1)}, s32[1,128]{1,0:T(1,128)}, u32[]{:S(2)}) copy-start(s32[1,128]{1,0:T(1,128)} %param.23) | copy-start | bytes 1540
  289.3 1.7 copy-start.1
  289.3 3.8 copy-start.28
  295.4 4.5 copy-start.10
  295.4 4.5 copy-start.12
  295.4 5.8 copy-start.25
  299.9 2.1 copy-start.21
  300.4 0.8 copy-start.9
  300.4 1.6 copy-start.35
  300.4 1.6 copy-start.30
  345.9 84.6 %reduce-scatter.16.cloned.1.call-start = ((), (), s32[]{:S(2)}) async-start(), calls=%async_computation.14 | async-start | bytes 1228800
  366.9 4.9 copy-start.6
  371.9 1.3 copy-start.4
  377.5 82.8 %reduce-scatter.10.cloned.1.call-start = ((), (), s32[]{:S(2)}) async-start(), calls=%async_computation.11 | async-start | bytes 2457600 | tf_op jit(solution)/shard_map/reduce_scatter | solution.py:211
  399.8 24.3 %copy-start.5 = (f32[2,32,10,768]{3,1,2,0:T(8,128)S(1)}, f32[2,32,10,768]{3,1,2,0:T(8,128)}, u32[]{:S(2)}) copy-start(f32[2,32,10,768]{3,1,2,0:T(8,128)} %copy-done.4) | copy-start | bytes 5898244
  424.1 3.1 copy-start.16
  424.1 4.1 copy-start.7
  427.2 1.0 copy-start.14
  432.3 29.9 %all-to-all-start.1 = ((bf16[8,2,10,768]{3,1,2,0:T(2,128)(2,1)}), bf16[8,2,10,768]{3,1,2,0:T(2,128)(2,1)}, u32[]{:S(2)}, u32[]{:S(2)}) async-start(bf16[8,2,10,768]{3,1,2,0:T(2,128)(2,1)} %copy.74), calls=%async_computation.1 | async-start | bytes 491520 | tf_op jit(solution)/shard_map/all_to_all | solution.py:190
  462.2 14.3 %all-to-all-start.3 = ((bf16[8,2,10,768]{3,1,2,0:T(2,128)(2,1)}), bf16[8,2,10,768]{3,1,2,0:T(2,128)(2,1)}, u32[]{:S(2)}, u32[]{:S(2)}) async-start(bf16[8,2,10,768]{3,1,2,0:T(2,128)(2,1)} %copy.78), calls=%async_computation.4 | async-start | bytes 491520 | tf_op jit(solution)/shard_map/all_to_all | solution.py:217
  467.7 66.5 %reduce-scatter.18.cloned.1.call-start = ((), (), s32[]{:S(2)}) async-start(), calls=%async_computation.15 | async-start | bytes 1966080
  473.3 9.9 %copy-start.26 = (f32[768]{0:T(1024)S(1)}, f32[768]{0:T(1024)}, u32[]{:S(2)}) copy-start(f32[768]{0:T(1024)} %param.17) | copy-start | bytes 9220
  483.2 5.4 copy-start.13
  487.8 0.7 copy-start.8
  495.5 2.9 copy-start.2
  495.5 3.1 copy-start.17
  495.5 3.1 copy-start.22
  498.7 3.0 copy-start.20
  499.9 1.8 copy-start.3
  505.8 101.9 %reduce-scatter.14.cloned.1.call-start = ((), (), s32[]{:S(2)}) async-start(), calls=%async_computation.13 | async-start | bytes 1327104 | tf_op jit(solution)/shard_map/reduce_scatter | solution.py:265
  508.5 27.7 %copy-start.27 = (f32[768]{0:T(1024)S(1)}, f32[768]{0:T(1024)}, u32[]{:S(2)}) copy-start(f32[768]{0:T(1024)} %param.16) | copy-start | bytes 9220
  508.5 27.7 %copy-start.32 = (f32[128]{0:T(128)S(1)}, f32[128]{0:T(128)}, u32[]{:S(2)}) copy-start(f32[128]{0:T(128)} %copy-done.31) | copy-start | bytes 1540
  508.5 175.8 %reduce-scatter.12.cloned.1.call-start = ((), (), s32[]{:S(2)}) async-start(), calls=%async_computation.12 | async-start | bytes 3981312 | tf_op jit(solution)/shard_map/reduce_scatter | solution.py:262
  540.3 2.1 copy-start.38
  540.3 179.8 %all-reduce.8.cloned.1.call-start = ((), (), s32[]{:S(2)}) async-start(), calls=%async_computation.16 | async-start | bytes 1179648 | tf_op jit(solution)/shard_map/psum | solution.py:279
  544.3 5.6 copy-start.15
  544.3 5.6 copy-start.19
  560.8 6.3 copy-start.11
  560.8 6.3 copy-start.23
  560.8 6.4 copy-start.24
  560.8 6.4 copy-start.33
  567.2 2.6 copy-start.29
  (1 other events, 0.6 us)
Sparse Core Ops, SparseCore 0:
  12.9 22.3 all-gather.2
  346.0 20.8 all-gather.4
  377.6 24.4 reduce-scatter.15
  430.6 29.6 reduce-scatter.9
  505.9 28.2 reduce-scatter.17
  537.9 64.0 reduce-scatter.13
  606.0 78.1 reduce-scatter.11
  686.9 33.1 all-reduce.7
where the time goes:
time: 738 us; the launch traced here: 731 us
  local copies, waits for them, and re-layouts  365 us (49%)
  waiting for transfers between devices  164 us (22%)
  blocking collectives  88.1 us (12%)
  matrix products  57.9 us (8%)
  other arithmetic  28.2 us (4%)
  between operations  15.8 us (2%)
  starting transfers between devices  10.7 us (1%)
    gather x2, local copies, waits for them, and re-layouts, forward_one_block(): scores = dots * score_scale + jnp.take(table_heads, columns, axis=1)  257 us
    reduce_scatter x1, waiting for transfers between devices, body(): lax.psum_scatter(qkv_part.astype(jnp.bfloat16), 'experts', scatter_dimens...  76.5 us
    unnamed x1, blocking collectives  37.3 us
    scatter x2, local copies, waits for them, and re-layouts, to_buckets(): return empty.at[routes, slot_ids].set(token_rows).reshape(expert_ranks, e...  36.2 us
    unnamed x89, local copies, waits for them, and re-layouts  25.4 us
    reduce_scatter x1, waiting for transfers between devices, body(): lax.psum_scatter(jnp.einsum('bxcf,xdf->bxcd', part_rows, expert_in, prefe...  23.8 us
    unnamed x10, waiting for transfers between devices  22.4 us
    all_to_all x1, blocking collectives, body(): lax.all_to_all(to_buckets(second_normed), 'experts', split_axis=0, concat...  20.9 us
  transfers between devices with their start and end apart: 10, of which 6 were waited for; matrix products, arithmetic and copies ran while one was open for 49% of the time, Pallas kernels for 0%

commit v1 on v0

v1 whole, which is shorter than its diff:
```python
import functools
import math

import jax
import jax.numpy as jnp
from jax import lax
from jax.experimental import pallas as pl
from jax.experimental.pallas import tpu as pltpu
from jax.sharding import PartitionSpec as P

norm_eps = 1e-06
f32 = jnp.float32
bf16 = jnp.bfloat16
NT = (((1,), (1,)), ((), ()))
TN = (((0,), (0,)), ((), ()))
VMEM_BYTES = 48 * 1024 * 1024


def rms_scale(values, gain):
    factor = lax.rsqrt(jnp.mean(values * values, axis=-1, keepdims=True) + norm_eps)
    return values * factor * gain


def dot(a, b, dims=(((1,), (0,)), ((), ()))):
    return lax.dot_general(a, b, dims, preferred_element_type=f32)


def lane_lookup(row, index):
    source = jnp.broadcast_to(row, index.shape)
    numbers = lax.GatherDimensionNumbers(
        offset_dims=(),
        collapsed_slice_dims=(1,),
        start_index_map=(1,),
        operand_batching_dims=(0,),
        start_indices_batching_dims=(0,),
    )
    return lax.gather(
        source,
        index[..., None],
        numbers,
        slice_sizes=(1, 1),
        mode=lax.GatherScatterMode.PROMISE_IN_BOUNDS,
    )


def forward_kernel(scale, step, q_ref, k_ref, v_ref, table_ref, ids_ref, att_ref, prob_ref):
    total = ids_ref.shape[0]
    keys = k_ref[0]
    values = v_ref[0]
    row = table_ref[0]

    @pl.loop(0, total // step)
    def _(index):
        rows = pl.ds(pl.multiple_of(index * step, step), step)
        scores = dot(q_ref[0, rows, :], keys, NT) * scale
        ids = ids_ref[rows, :].astype(f32).astype(jnp.int32)
        bias = [lane_lookup(row, ids[:, at : at + 128]) for at in range(0, total, 128)]
        scores = scores + jnp.concatenate(bias, axis=1)
        expons = jnp.exp(scores - jnp.max(scores, axis=1, keepdims=True))
        probs = (expons / jnp.sum(expons, axis=1, keepdims=True)).astype(bf16)
        prob_ref[0, rows, :] = probs
        att_ref[0, rows, :] = dot(probs, values).astype(bf16)


def backward_kernel(
    scale, step, q_ref, k_ref, v_ref, att_ref, grad_ref, prob_ref, dq_ref, dk_ref, dv_ref, ds_ref,
    dk_sum, dv_sum,
):
    total = q_ref.shape[1]
    keys = k_ref[0]
    values = v_ref[0]
    dk_sum[...] = jnp.zeros_like(dk_sum)
    dv_sum[...] = jnp.zeros_like(dv_sum)

    @pl.loop(0, total // step)
    def _(index):
        rows = pl.ds(pl.multiple_of(index * step, step), step)
        grad = grad_ref[0, rows, :]
        probs = prob_ref[0, rows, :]
        delta = jnp.sum(
            grad.astype(f32) * att_ref[0, rows, :].astype(f32), axis=1, keepdims=True
        )
        d_scores = (probs.astype(f32) * (dot(grad, values, NT) - delta)).astype(bf16)
        ds_ref[0, rows, :] = d_scores
        dq_ref[0, rows, :] = (dot(d_scores, keys) * scale).astype(bf16)
        dk_sum[...] += dot(d_scores, q_ref[0, rows, :], TN)
        dv_sum[...] += dot(probs, grad, TN)

    dk_ref[0] = (dk_sum[...] * scale).astype(bf16)
    dv_ref[0] = dv_sum[...].astype(bf16)


def table_kernel(buckets, ds_ref, ids_ref, out_ref):
    total = ids_ref.shape[0]
    width = ids_ref.shape[1]
    group = 64

    def one_bucket(bucket, _):
        wanted = bucket.astype(f32).astype(bf16)

        def one_group(index, acc):
            rows = pl.ds(pl.multiple_of(index * group, group), group)
            picked = jnp.where(ids_ref[rows, :] == wanted, ds_ref[0, rows, :], jnp.zeros((), bf16))
            part = picked[0:16] + picked[16:32]
            for at in range(32, group, 16):
                part = part + picked[at : at + 16]
            return acc + part.astype(f32)

        acc = lax.fori_loop(0, total // group, one_group, jnp.zeros((16, width), f32), unroll=True)
        out_ref[0, pl.ds(bucket, 1), :] = jnp.sum(acc, axis=0, keepdims=True)
        return 0

    lax.fori_loop(0, buckets, one_bucket, 0)


def head_spec(rows, columns):
    return pl.BlockSpec((1, rows, columns), lambda h: (h, 0, 0))


def attend(q, k, v, table, ids):
    heads, total, size = q.shape
    scale = 1.0 / math.sqrt(size)
    return pl.pallas_call(
        functools.partial(forward_kernel, scale, 128),
        grid=(heads,),
        in_specs=[head_spec(total, size)] * 3
        + [head_spec(1, 128), pl.BlockSpec((total, total), lambda h: (0, 0))],
        out_specs=[head_spec(total, size), head_spec(total, total)],
        out_shape=[
            jax.ShapeDtypeStruct((heads, total, size), bf16),
            jax.ShapeDtypeStruct((heads, total, total), bf16),
        ],
        cost_estimate=pl.CostEstimate(
            flops=4 * heads * total * total * size,
            bytes_accessed=4 * heads * total * total,
            transcendentals=heads * total * total,
        ),
        compiler_params=pltpu.CompilerParams(vmem_limit_bytes=VMEM_BYTES),
        name="attend",
    )(q, k, v, table, ids)


def attend_back(q, k, v, att, grad, probs):
    heads, total, size = q.shape
    scale = 1.0 / math.sqrt(size)
    small = jax.ShapeDtypeStruct((heads, total, size), bf16)
    return pl.pallas_call(
        functools.partial(backward_kernel, scale, 128),
        grid=(heads,),
        in_specs=[head_spec(total, size)] * 5 + [head_spec(total, total)],
        out_specs=[head_spec(total, size)] * 3 + [head_spec(total, total)],
        out_shape=[small] * 3 + [jax.ShapeDtypeStruct((heads, total, total), bf16)],
        scratch_shapes=[pltpu.VMEM((total, size), f32)] * 2,
        cost_estimate=pl.CostEstimate(
            flops=8 * heads * total * total * size,
            bytes_accessed=8 * heads * total * total,
            transcendentals=0,
        ),
        compiler_params=pltpu.CompilerParams(vmem_limit_bytes=VMEM_BYTES),
        name="attend_back",
    )(q, k, v, att, grad, probs)


def table_sums(d_scores, ids, buckets):
    heads, total, _ = d_scores.shape
    sums = pl.pallas_call(
        functools.partial(table_kernel, buckets),
        grid=(heads,),
        in_specs=[head_spec(total, total), pl.BlockSpec((total, total), lambda h: (0, 0))],
        out_specs=head_spec(buckets, total),
        out_shape=jax.ShapeDtypeStruct((heads, buckets, total), f32),
        cost_estimate=pl.CostEstimate(
            flops=64 * heads * total * total,
            bytes_accessed=4 * heads * total * total,
            transcendentals=0,
        ),
        compiler_params=pltpu.CompilerParams(vmem_limit_bytes=VMEM_BYTES),
        name="table_sums",
    )(d_scores, ids)
    return jnp.sum(sums, axis=2)


def body(
    block_input,
    first_gain,
    second_gain,
    qkv_weight,
    out_weight,
    rel_table,
    bucket_ids,
    expert_route,
    expert_slot,
    gate_value,
    expert_in,
    expert_down,
    upstream,
):
    ranks = lax.axis_size("context")
    me = lax.axis_index("context")
    expert_ranks = lax.axis_size("experts")
    local_rows, width = block_input.shape[1:]
    buckets, heads = rel_table.shape
    size = width // heads
    total = bucket_ids.shape[1]
    group = -(-heads // ranks)
    spare = group * ranks - heads
    share = group * size
    columns = width // ranks
    experts_local = expert_in.shape[0]
    experts_total = experts_local * expert_ranks
    capacity = max(4, 4 * local_rows // (3 * experts_total))
    slots = experts_total * capacity
    local_slots = experts_local * capacity

    features = block_input[0].astype(f32)
    gates = gate_value[0][:, None]
    grad_top = upstream[0].astype(f32)
    place = expert_route[0] * capacity + expert_slot[0]
    chosen = (place[None, :] == jnp.arange(slots, dtype=jnp.int32)[:, None]).astype(bf16)

    def send_rows(rows):
        spread = dot(chosen, rows).astype(bf16).reshape(expert_ranks, local_slots, -1)
        arrived = lax.all_to_all(spread, "experts", split_axis=0, concat_axis=0, tiled=True)
        return lax.all_gather(arrived, "context", axis=0, tiled=True)

    shared = lax.all_gather(
        jnp.concatenate([block_input[0], bucket_ids.astype(bf16)], axis=1),
        "context",
        axis=0,
        tiled=True,
    )
    all_features = shared[:, :width].astype(f32)
    ids = shared[:, width:]
    grad_rows = send_rows((gates * grad_top).astype(bf16))
    normed = rms_scale(all_features, first_gain).astype(bf16)
    weight = jnp.pad(
        qkv_weight.reshape(width, 3, heads * size), ((0, 0), (0, 0), (0, spare * size))
    )
    my_weight = lax.dynamic_slice_in_dim(weight, me * share, share, 2).reshape(width, 3 * share)
    qkv = (
        dot(normed, my_weight)
        .astype(bf16)
        .reshape(total, 3, group, size)
        .transpose(1, 2, 0, 3)
    )
    q, k, v = qkv[0], qkv[1], qkv[2]
    table = jnp.pad(rel_table.T, ((0, spare), (0, 128 - buckets)))
    my_table = lax.dynamic_slice_in_dim(table, me * group, group, 0)[:, None, :]
    att, probs = attend(q, k, v, my_table, ids)
    all_att = lax.all_gather(
        att.transpose(1, 0, 2).reshape(total, share), "context", axis=0, tiled=False
    )
    all_att = all_att.transpose(1, 0, 2).reshape(total, ranks * share)[:, :width]
    attended = lax.dynamic_slice_in_dim(all_att, me * local_rows, local_rows, 0)
    middle = features + dot(attended, out_weight)
    second_normed = rms_scale(middle, second_gain)

    high_wide = lax.reduce_precision(second_normed, 8, 7)
    high = high_wide.astype(bf16)
    low = (second_normed - high_wide).astype(bf16)
    gathered = send_rows(jnp.concatenate([high, low], axis=1))

    def by_expert(rows):
        rows = rows.reshape(ranks * expert_ranks, experts_local, capacity, -1)
        return rows.transpose(1, 0, 2, 3).reshape(
            experts_local, ranks * expert_ranks * capacity, -1
        )

    def by_block(rows):
        rows = rows.reshape(experts_local, ranks, expert_ranks, capacity, -1)
        return rows.transpose(1, 2, 0, 3, 4).reshape(ranks, expert_ranks, local_slots, -1)

    wide = by_expert(gathered)
    grads = by_expert(grad_rows)
    high_rows, low_rows = wide[:, :, :width], wide[:, :, width:]
    batched = functools.partial(jnp.einsum, preferred_element_type=f32)
    pre_act = batched("xnd,xdf->xnf", high_rows, expert_in) + batched(
        "xnd,xdf->xnf", low_rows, expert_in
    )
    hidden = jnp.maximum(pre_act, 0.0).astype(bf16)
    hidden_grad = batched("xnd,xfd->xnf", grads, expert_down)
    pre_grad = jnp.where(pre_act > 0.0, hidden_grad, 0.0).astype(bf16)
    forward_out = batched("xnf,xfd->xnd", hidden, expert_down).astype(bf16)
    back_in = batched("xnf,xdf->xnd", pre_grad, expert_in).astype(bf16)
    partial = by_block(jnp.concatenate([forward_out, back_in], axis=2))
    pieces = lax.all_to_all(partial, "context", split_axis=0, concat_axis=0, tiled=True)
    summed = jnp.sum(pieces.astype(f32), axis=0).astype(bf16)
    returned = lax.all_to_all(summed, "experts", split_axis=0, concat_axis=0, tiled=True)
    picked = dot(chosen, returned.reshape(slots, 2 * width), TN)
    inner_grad = batched("xnd,xnf->xdf", high_rows, pre_grad)
    down_grad = batched("xnf,xnd->xfd", hidden, grads)
    block_output = (middle + gates * picked[:, :width]).astype(bf16)[None]

    _, second_pull = jax.vjp(rms_scale, middle, second_gain)
    d_middle_norm, second_part = second_pull(picked[:, width:])
    d_middle = grad_top + d_middle_norm
    all_d_middle = lax.all_gather(d_middle.astype(bf16), "context", axis=0, tiled=True)

    out_rows = jnp.pad(out_weight, ((0, spare * size), (0, 0)))
    my_out = lax.dynamic_slice_in_dim(out_rows, me * share, share, 0)
    d_att = (
        dot(all_d_middle, my_out, NT).astype(bf16).reshape(total, group, size).transpose(1, 0, 2)
    )
    dq, dk, dv, d_scores = attend_back(q, k, v, att, d_att, probs)
    d_qkv = jnp.stack([dq, dk, dv]).transpose(2, 0, 1, 3).reshape(total, 3 * share)
    own = lax.all_to_all(
        d_qkv.reshape(ranks, local_rows, 3 * share),
        "context",
        split_axis=0,
        concat_axis=0,
        tiled=True,
    )
    own = own.reshape(ranks, local_rows, 3, share).transpose(1, 2, 0, 3)
    own = own.reshape(local_rows, 3, ranks * share)[:, :, :width].reshape(local_rows, 3 * width)
    d_first = dot(own, qkv_weight, NT)
    _, first_pull = jax.vjp(rms_scale, features, first_gain)
    d_input_norm, first_part = first_pull(d_first)
    input_grad = (d_middle + d_input_norm)[None]

    my_d_middle = lax.dynamic_slice_in_dim(all_d_middle, me * columns, columns, 1)
    qkv_part = dot(normed, d_qkv, TN)
    proj_part = dot(all_att, my_d_middle, TN)
    table_part = table_sums(d_scores, ids, buckets).T
    wide_part = jnp.concatenate([qkv_part, proj_part], axis=1).astype(bf16)
    grad_width = 3 * share + columns
    rows_out = width // expert_ranks
    table_out = buckets // expert_ranks
    small = jnp.concatenate(
        [
            first_part.reshape(expert_ranks, rows_out),
            second_part.reshape(expert_ranks, rows_out),
            table_part.reshape(expert_ranks, table_out * group),
        ],
        axis=1,
    ).astype(bf16)
    small = jnp.pad(small, ((0, 0), (0, grad_width - small.shape[1])))
    wide_part = jnp.concatenate(
        [wide_part.reshape(expert_ranks, rows_out, grad_width), small[:, None, :]], axis=1
    )
    sums = lax.all_to_all(wide_part, "experts", split_axis=0, concat_axis=0, tiled=True)
    sums = jnp.sum(sums.astype(f32), axis=0).astype(bf16)
    full = lax.all_gather(sums, "context", axis=0, tiled=False).astype(f32)
    qkv_grad = full[:, :rows_out, : 3 * share].reshape(ranks, rows_out, 3, share)
    qkv_grad = qkv_grad.transpose(1, 2, 0, 3).reshape(rows_out, 3, ranks * share)
    qkv_grad = qkv_grad[:, :, :width].reshape(rows_out, 3 * width)
    proj_grad = full[:, :rows_out, 3 * share :].transpose(1, 0, 2).reshape(rows_out, width)
    last = full[:, rows_out]
    first_grad = jnp.sum(last[:, :rows_out], axis=0)
    second_grad = jnp.sum(last[:, rows_out : 2 * rows_out], axis=0)
    table_grad = last[:, 2 * rows_out : 2 * rows_out + table_out * group]
    table_grad = table_grad.reshape(ranks, table_out, group).transpose(1, 0, 2)
    table_grad = table_grad.reshape(table_out, ranks * group)[:, :heads]
    return (
        block_output,
        input_grad,
        qkv_grad,
        proj_grad,
        first_grad,
        second_grad,
        table_grad,
        inner_grad,
        down_grad,
    )


def solution(mesh):
    placed = (
        P("experts", "context", None),
        P(),
        P(),
        P(),
        P(),
        P(),
        P("context", None),
        P("experts", "context"),
        P("experts", "context"),
        P("experts", "context"),
        P("experts", None, "context"),
        P("experts", "context", None),
        P("experts", "context", None),
    )
    return jax.shard_map(
        body,
        mesh=mesh,
        in_specs=placed,
        out_specs=(
            P("experts", "context", None),
            P("experts", "context", None),
            P("experts", None),
            P("experts", None),
            P("experts"),
            P("experts"),
            P("experts", None),
            P("experts", None, "context"),
            P("experts", "context", None),
        ),
        check_vma=False,
    )
```

time: 738 us -> 296 us (0.40)
  local copies, waits for them, and re-layouts: 365 us -> 52.7 us
  waiting for transfers between devices: 164 us -> 54.5 us
  matrix products: 57.9 us -> 29.5 us
  Pallas kernels: 0 us -> 21.5 us
  other arithmetic: 28.2 us -> 13.7 us
    gather x4 -> x0, local copies, waits for them, and re-layouts: 264 us -> none  [the longest x2 257 us: forward_one_block(): scores = dots * score_scale + jnp.take(table_heads, columns, axis=1)]
    reduce_scatter x3 -> x0, waiting for transfers between devices: 100 us -> none  [the longest x1 76.5 us: body(): lax.psum_scatter(qkv_part.astype(jnp.bfloat16), 'experts', scatter_dimens...]
    unnamed x1 -> x0, blocking collectives: 37.3 us -> none
    scatter x2 -> x0, local copies, waits for them, and re-layouts: 36.2 us -> none  [to_buckets(): return empty.at[routes, slot_ids].set(token_rows).reshape(expert_ranks, e...]
    dot_general x19 -> x16, matrix products: 57.9 us -> 29.5 us  [the longest x9 16 us: dot(): return lax.dot_general(a, b, dims, preferred_element_type=f32)]
    all_to_all x2 -> x3, blocking collectives: 35.4 us -> 62.7 us  [the longest x2 35.8 us: send_rows(): lax.all_to_all(spread, 'experts', split_axis=0, concat_axis=0, tiled=True)]
    all_to_all x1 -> x2, waiting for transfers between devices: 0.14 us -> 27.2 us  [the longest x1 21 us: body(): lax.all_to_all(wide_part, 'experts', split_axis=0, concat_axis=0, tiled=T...]
    all_gather x1 -> x4, blocking collectives: 8.59 us -> 32.7 us  [the longest x1 8.92 us: send_rows(): return lax.all_gather(arrived, 'context', axis=0, tiled=True)]
  transfers between devices with their start and end apart: 10 -> 5, of which waited for: 6 -> 4; matrix products, arithmetic and copies ran while one was open for 49% -> 9% of each run, Pallas kernels for 0% -> 0%
where the time goes in v1:
time: 296 us; the launch traced here: 294 us
  blocking collectives  95.4 us (32%)
  waiting for transfers between devices  54.5 us (18%)
  local copies, waits for them, and re-layouts  52.7 us (18%)
  matrix products  29.5 us (10%)
  Pallas kernels  21.5 us (7%)
  between operations  14.7 us (5%)
  other arithmetic  13.7 us (5%)
  starting transfers between devices  12.2 us (4%)
    all_to_all x2, blocking collectives, send_rows(): lax.all_to_all(spread, 'experts', split_axis=0, concat_axis=0, tiled=True)  35.8 us
    all_to_all x1, blocking collectives, body(): lax.all_to_all(partial, 'context', split_axis=0, concat_axis=0, tiled=True)  26.8 us
    all_to_all x1, waiting for transfers between devices, body(): lax.all_to_all(wide_part, 'experts', split_axis=0, concat_axis=0, tiled=T...  21 us
    dot_general x9, matrix products, dot(): return lax.dot_general(a, b, dims, preferred_element_type=f32)  16 us
    all_to_all x1, waiting for transfers between devices, body(): lax.all_to_all(summed, 'experts', split_axis=0, concat_axis=0, tiled=True)  14 us
    all_gather x1, waiting for transfers between devices, body(): lax.all_gather(jnp.concatenate([block_input[0], bucket_ids.astype(bf16)],...  13.2 us
    unnamed x73, local copies, waits for them, and re-layouts  12.3 us
    all_gather x1, blocking collectives, send_rows(): return lax.all_gather(arrived, 'context', axis=0, tiled=True)  8.92 us
  transfers between devices with their start and end apart: 5, of which 4 were waited for; matrix products, arithmetic and copies ran while one was open for 9% of the time, Pallas kernels for 0%

profile of v1, /device:TPU:0, one launch (start us, length us, event | category | flops | bytes accessed | tf_op | source)
XLA Modules:
  0.0 294.1 jit_solution(8471031958425605290)
XLA Ops:
  8.4 1.7 pad_maximum_fusion.2
  10.9 5.8 %copy.130 = bf16[768,2304]{0,1:T(8,128)(2,1)} copy(bf16[768,2304]{1,0:T(8,128)(2,1)} %param.16) | data formatting | bytes 7077888 | tf_op args[3]
  16.6 1.2 constant_dynamic-slice_fusion
  17.9 13.2 %all-gather.5.cloned.1.call-done = bf16[512,1280]{1,0:T(8,128)(2,1)} async-done(((bf16[128,1280]{1,0:T(8,128)(2,1)}), bf16[512,1280]{1,0:T(8,128)(2,1)}) %all-gather.5.cloned.1.call-update) | async-done | bytes 1310736 | tf_op jit(solution)/shard_map/all_gather | solution.py:226
  31.1 1.4 fusion
  32.5 2.7 convolution_convert_fusion.4
  35.2 2.3 copy.131
  37.4 1.3 slice_bitcast_fusion
  38.8 1.4 slice.64.ids_ref
  40.2 7.0 %attend.1 = (bf16[3,512,64]{2,1,0:T(8,128)(2,1)S(1)}, bf16[3,512,512]{2,1,0:T(8,128)(2,1)S(1)}) custom-call(bf16[3,512,64]{2,1,0:T(8,128)(2,1)S(1)} %get-tuple-element.33.q_ref, bf16[3,512,64]{2,1,0:T(8,128)(2,1)S(1)} %get-tuple-element.32.k_ref, bf16[3,512,64]{2,1,0:T(8,128)(2,1)S(1)} %get-tuple-element.31.v_ref, ...), custom_call_target="tpu_custom_call" | custom-call | flops 201326592 | bytes 3145728 | tf_op jit(solution)/shard_map/attend/pallas_call | solution.py:123
  49.1 1.8 copy.132
  50.9 8.8 %all_gather.22 = bf16[4,512,192]{1,2,0:T(8,128)(2,1)S(1)} all-gather(bf16[1,512,192]{1,2,0:T(8,128)(2,1)} %bitcast.134), channel_id=1, replica_groups=mesh['experts'=8,'context'=4] {'context'}, dimensions={0}, use_global_device_ids=true | all-gather | bytes 983040 | tf_op jit(solution)/shard_map/all_gather | solution.py:250
  59.8 2.0 multiply_reduce_fusion.2
  63.7 2.0 reshape.152
  65.7 22.6 %all_to_all.30 = bf16[8,20,1536]{2,1,0:T(8,128)(2,1)S(1)} all-to-all(bf16[8,20,1536]{2,1,0:T(8,128)(2,1)} %reshape.152), channel_id=1, replica_groups=mesh['experts'=8,'context'=4] {'experts'}, dimensions={0} | all-to-all | bytes 983040 | tf_op jit(solution)/shard_map/all_to_all | solution.py:223
  89.2 1.9 convolution_convert_fusion.6
  91.1 1.7 reshape.155
  92.8 13.3 %all_to_all.31 = bf16[8,20,768]{2,1,0:T(8,128)(2,1)S(1)} all-to-all(bf16[8,20,768]{2,1,0:T(8,128)(2,1)} %reshape.155), channel_id=1, replica_groups=mesh['experts'=8,'context'=4] {'experts'}, dimensions={0} | all-to-all | bytes 491520 | tf_op jit(solution)/shard_map/all_to_all | solution.py:223
  106.2 8.9 %all_gather.24 = bf16[32,20,768]{2,0,1:T(8,128)(2,1)S(1)} all-gather(bf16[8,20,768]{2,0,1:T(8,128)(2,1)S(1)} %copy.137), channel_id=1, replica_groups=mesh['experts'=8,'context'=4] {'context'}, dimensions={0}, use_global_device_ids=true | all-gather | bytes 1228800 | tf_op jit(solution)/shard_map/all_gather | solution.py:224
  115.1 2.0 copy.138
  117.0 3.6 %copy.134 = bf16[2,32,10,1536]{3,0,2,1:T(2,128)(2,1)S(1)} copy(bf16[2,32,10,1536]{3,1,2,0:T(8,128)(2,1)} %bitcast.129) | data formatting | bytes 3932160 | tf_op jit(solution)/shard_map/transpose | solution.py:265
  120.6 1.4 fusion.54
  128.1 2.0 copy.140
  130.5 26.8 %all_to_all.32 = bf16[4,8,20,1536]{3,1,2,0:T(8,128)(2,1)S(1)} all-to-all(bf16[4,8,20,1536]{3,1,2,0:T(8,128)(2,1)S(1)} %bitcast.116), channel_id=1, replica_groups=mesh['experts'=8,'context'=4] {'context'}, dimensions={0} | all-to-all | bytes 3932160 | tf_op jit(solution)/shard_map/all_to_all | solution.py:286
  158.5 2.1 copy.142
  160.6 4.4 %all-to-all-start.3 = ((bf16[8,20,1536]{2,1,0:T(8,128)(2,1)}), bf16[8,20,1536]{2,1,0:T(8,128)(2,1)}, u32[]{:S(2)}, u32[]{:S(2)}) async-start(bf16[8,20,1536]{2,1,0:T(8,128)(2,1)} %copy.142), calls=%async_computation.3 | async-start | bytes 1179648 | tf_op jit(solution)/shard_map/all_to_all | solution.py:288
  166.6 14.0 %all-to-all-done.3 = bf16[8,20,1536]{2,1,0:T(8,128)(2,1)} async-done(((bf16[8,20,1536]{2,1,0:T(8,128)(2,1)}), bf16[8,20,1536]{2,1,0:T(8,128)(2,1)}, u32[]{:S(2)}, u32[]{:S(2)}) %all-to-all-start.3) | async-done | bytes 491552 | tf_op jit(solution)/shard_map/all_to_all | solution.py:288
  182.5 8.1 %all_gather.25 = bf16[512,768]{1,0:T(8,128)(2,1)S(1)} all-gather(bf16[128,768]{1,0:T(8,128)(2,1)S(1)} %fusion.53), channel_id=1, replica_groups=mesh['experts'=8,'context'=4] {'context'}, dimensions={0}, use_global_device_ids=true | all-gather | bytes 983040 | tf_op jit(solution)/shard_map/all_gather | solution.py:297
  191.5 1.4 convolution_convert_fusion.7
  195.8 6.7 %attend_back.1 = (bf16[3,512,64]{2,1,0:T(8,128)(2,1)S(1)}, bf16[3,512,64]{2,1,0:T(8,128)(2,1)S(1)}, bf16[3,512,64]{2,1,0:T(8,128)(2,1)S(1)}, bf16[3,512,512]{2,1,0:T(8,128)(2,1)S(1)}) custom-call(bf16[3,512,64]{2,1,0:T(8,128)(2,1)S(1)} %copy-done.5, bf16[3,512,64]{2,1,0:T(8,128)(2,1)S(1)} %copy-done.3, bf16[3,512,64]{2,1,0:T(8,128)(2,1)S(1)} %get-tuple-element.31.v_ref, ...), custom_call_target="tpu_custom_call" | custom-call | flops 402653184 | bytes 6291456 | tf_op jit(solution)/shard_map/attend_back/pallas_call | solution.py:147
  202.5 7.8 %table_sums.1 = f32[3,32,512]{2,1,0:T(8,128)S(1)} custom-call(bf16[3,512,512]{2,1,0:T(8,128)(2,1)S(1)} %get-tuple-element.20.ds_ref, bf16[512,512]{1,0:T(8,128)(2,1)S(1)} %slice.64.ids_ref), custom_call_target="tpu_custom_call" | custom-call | flops 50331648 | bytes 3145728 | tf_op jit(solution)/shard_map/table_sums/pallas_call | solution.py:166
  210.3 1.3 maximum_bitcast_fusion
  211.6 1.5 copy.144
  214.5 3.5 %all-to-all-start.4 = ((bf16[4,128,576]{1,2,0:T(8,128)(2,1)}), bf16[4,128,576]{1,2,0:T(8,128)(2,1)S(1)}, u32[]{:S(2)}, u32[]{:S(2)}) async-start(bf16[4,128,576]{1,2,0:T(8,128)(2,1)} %copy.145), calls=%async_computation.4 | async-start | bytes 1179648 | tf_op jit(solution)/shard_map/all_to_all | solution.py:306
  218.0 1.5 convolution_convert_fusion.5
  219.5 1.8 convolution_convert_fusion.1
  221.3 6.3 %all-to-all-done.4 = bf16[4,128,576]{1,2,0:T(8,128)(2,1)S(1)} async-done(((bf16[4,128,576]{1,2,0:T(8,128)(2,1)}), bf16[4,128,576]{1,2,0:T(8,128)(2,1)S(1)}, u32[]{:S(2)}, u32[]{:S(2)}) %all-to-all-start.4) | async-done | bytes 589856 | tf_op jit(solution)/shard_map/all_to_all | solution.py:306
  227.6 3.4 %fusion.19 = (bf16[768]{0:T(1024)(128)(2,1)S(1)}, f32[128]{0:T(128)S(1)}, f32[128,768]{1,0:T(8,128)S(1)}) fusion(f32[128]{0:T(128)S(1)} %fusion.49, bf16[1,128,768]{2,1,0:T(8,128)(2,1)S(1)} %copy-done.17, f32[768]{0:T(1024)S(1)} %copy-done.31, bf16[128,2304]{0,1:T(8,128)(2,1)S(1)} %bitcast.128, bf16[768,2304]{1,0:T(8,128)(2,1)} %param.16), kind=kOutput, calls=%fused_computation.49 | convolution fusion | flops 453672064 | bytes 4724224 | tf_op jit(solution)/shard_map/dot_general | solution.py:25
  231.2 2.6 pad_maximum_fusion.1
  233.8 4.2 %all-to-all-start.5 = ((bf16[8,97,768]{2,1,0:T(8,128)(2,1)}), bf16[8,97,768]{2,1,0:T(8,128)(2,1)}, u32[]{:S(2)}, u32[]{:S(2)}) async-start(bf16[8,97,768]{2,1,0:T(8,128)(2,1)} %pad_maximum_fusion.1), calls=%async_computation.5 | async-start | bytes 2555904 | tf_op jit(solution)/shard_map/all_to_all | solution.py:340
  238.1 5.0 %fusion.8 = f32[2,768,768]{2,1,0:T(8,128)} fusion(bf16[2,320,768]{2,0,1:T(2,128)(2,1)S(1)} %bitcast.124, bf16[2,320,768]{2,1,0:T(8,128)(2,1)} %copy-done.26), kind=kOutput, calls=%fused_computation.28 | convolution fusion | flops 756449280 | bytes 6684672 | tf_op jit(solution)/shard_map/xnf,xnd->xfd/dot_general | solution.py:291
  243.0 3.6 %fusion.4 = f32[2,768,768]{2,1,0:T(8,128)} fusion(bf16[2,320,768]{2,1,0:T(8,128)(2,1)S(1)} %copy-done.28, bf16[2,320,768]{2,0,1:T(2,128)(2,1)S(1)} %copy-done.14), kind=kOutput, calls=%fused_computation.24 | convolution fusion | flops 754974720 | bytes 6684672 | tf_op jit(solution)/shard_map/xnd,xnf->xdf/dot_general | solution.py:290
  247.8 21.0 %all-to-all-done.5 = bf16[8,97,768]{2,1,0:T(8,128)(2,1)} async-done(((bf16[8,97,768]{2,1,0:T(8,128)(2,1)}), bf16[8,97,768]{2,1,0:T(8,128)(2,1)}, u32[]{:S(2)}, u32[]{:S(2)}) %all-to-all-start.5) | async-done | bytes 1191968 | tf_op jit(solution)/shard_map/all_to_all | solution.py:340
  268.8 1.5 reduce_sum.143
  270.3 6.9 %all-gather.1 = bf16[4,97,768]{2,1,0:T(8,128)(2,1)S(1)} all-gather(bf16[1,97,768]{2,1,0:T(8,128)(2,1)S(1)} %bitcast.135), channel_id=2, replica_groups=mesh['experts'=8,'context'=4] {'context'}, dimensions={0}, use_global_device_ids=true | all-gather | bytes 744960 | tf_op jit(solution)/shard_map/all_gather | solution.py:342
  280.2 1.9 copy.159
  282.0 1.5 copy.153
  283.6 2.9 reshape_reshape.11
  (127 shorter events, 28.0 us)
Async XLA Ops:
  7.2 114.9 %copy-start = (bf16[2,768,768]{2,1,0:T(8,128)(2,1)S(1)}, bf16[2,768,768]{2,1,0:T(8,128)(2,1)}, u32[]{:S(2)}) copy-start(bf16[2,768,768]{2,1,0:T(8,128)(2,1)} %param.23) | copy-start | bytes 7077892
  7.2 23.9 %all-gather.5.cloned.1.call-start = ((), (), s32[]{:S(2)}) async-start(), calls=%async_computation.6 | async-start | bytes 1638400 | tf_op jit(solution)/shard_map/all_gather | solution.py:226
  10.1 107.0 %all-gather.7.cloned.1.call-start = ((), (), s32[]{:S(2)}) async-start(), calls=%async_computation.7 | async-start | bytes 2457600 | tf_op jit(solution)/shard_map/all_gather | solution.py:224
  10.8 7.0 %copy-start.34 = (s32[1,128]{1,0:T(1,128)S(1)}, s32[1,128]{1,0:T(1,128)}, u32[]{:S(2)}) copy-start(s32[1,128]{1,0:T(1,128)} %param.21) | copy-start | bytes 1540
  10.8 7.0 %copy-start.35 = (s32[1,128]{1,0:T(1,128)S(1)}, s32[1,128]{1,0:T(1,128)}, u32[]{:S(2)}) copy-start(s32[1,128]{1,0:T(1,128)} %param.20) | copy-start | bytes 1540
  16.6 15.9 %copy-start.31 = (f32[768]{0:T(1024)S(1)}, f32[768]{0:T(1024)}, u32[]{:S(2)}) copy-start(f32[768]{0:T(1024)} %param.14) | copy-start | bytes 9220
  38.8 1.4 copy-start.2
  38.8 8.4 %copy-start.4 = (bf16[3,512,64]{2,1,0:T(8,128)(2,1)}, bf16[3,512,64]{2,1,0:T(8,128)(2,1)S(1)}, u32[]{:S(2)}) copy-start(bf16[3,512,64]{2,1,0:T(8,128)(2,1)S(1)} %get-tuple-element.33.q_ref) | copy-start | bytes 589828
  38.8 21.0 %copy-start.17 = (bf16[1,128,768]{2,1,0:T(8,128)(2,1)S(1)}, bf16[1,128,768]{2,1,0:T(8,128)(2,1)}, u32[]{:S(2)}) copy-start(bf16[1,128,768]{2,1,0:T(8,128)(2,1)} %param.13) | copy-start | bytes 589828
  47.2 1.1 copy-start.6
  48.3 0.8 copy-start.7
  49.1 13.4 %copy-start.30 = (f32[768]{0:T(1024)S(1)}, f32[768]{0:T(1024)}, u32[]{:S(2)}) copy-start(f32[768]{0:T(1024)} %param.15) | copy-start | bytes 9220
  59.7 2.9 copy-start.19
  61.8 0.8 copy-start.10
  63.7 25.5 %copy-start.32 = (f32[1,128]{1,0:T(1,128)S(1)}, f32[1,128]{1,0:T(1,128)}, u32[]{:S(2)}) copy-start(f32[1,128]{1,0:T(1,128)} %param.22) | copy-start | bytes 1540
  122.0 1.0 copy-start.13
  123.0 1.2 copy-start.21
  123.0 2.0 copy-start.33
  124.1 2.9 copy-start.26
  126.0 1.0 copy-start.27
  158.5 6.7 %copy-start.23 = (bf16[512,1280]{1,0:T(8,128)(2,1)S(1)}, bf16[512,1280]{1,0:T(8,128)(2,1)}, u32[]{:S(2)}) copy-start(bf16[512,1280]{1,0:T(8,128)(2,1)} %all-gather.5.cloned.1.call-done) | copy-start | bytes 3932164
  160.6 20.0 %all-to-all-start.3 = ((bf16[8,20,1536]{2,1,0:T(8,128)(2,1)}), bf16[8,20,1536]{2,1,0:T(8,128)(2,1)}, u32[]{:S(2)}, u32[]{:S(2)}) async-start(bf16[8,20,1536]{2,1,0:T(8,128)(2,1)} %copy.142), calls=%async_computation.3 | async-start | bytes 1179648 | tf_op jit(solution)/shard_map/all_to_all | solution.py:288
  165.4 16.7 %copy-start.11 = (f32[128,768]{1,0:T(8,128)S(1)}, f32[128,768]{1,0:T(8,128)}, u32[]{:S(2)}) copy-start(f32[128,768]{1,0:T(8,128)} %copy-done.10) | copy-start | bytes 1179652
  166.6 15.7 %copy-start.24 = (bf16[1,128,768]{2,1,0:T(8,128)(2,1)S(1)}, bf16[1,128,768]{2,1,0:T(8,128)(2,1)}, u32[]{:S(2)}) copy-start(bf16[1,128,768]{2,1,0:T(8,128)(2,1)} %param.25) | copy-start | bytes 589828
  182.1 10.8 %copy-start.15 = (f32[128,1536]{1,0:T(8,128)}, f32[128,1536]{1,0:T(8,128)S(1)}, u32[]{:S(2)}) copy-start(f32[128,1536]{1,0:T(8,128)S(1)} %fusion.35) | copy-start | bytes 2359300
  182.4 11.4 %copy-start.3 = (bf16[3,512,64]{2,1,0:T(8,128)(2,1)S(1)}, bf16[3,512,64]{2,1,0:T(8,128)(2,1)}, u32[]{:S(2)}) copy-start(bf16[3,512,64]{2,1,0:T(8,128)(2,1)} %copy-done.2) | copy-start | bytes 589828
  182.4 11.4 %copy-start.5 = (bf16[3,512,64]{2,1,0:T(8,128)(2,1)S(1)}, bf16[3,512,64]{2,1,0:T(8,128)(2,1)}, u32[]{:S(2)}) copy-start(bf16[3,512,64]{2,1,0:T(8,128)(2,1)} %copy-done.4) | copy-start | bytes 589828
  190.6 0.9 copy-start.18
  193.8 1.0 copy-start.8
  194.8 1.0 copy-start.9
  213.2 4.8 %copy-start.20 = (bf16[4,512,192]{1,2,0:T(8,128)(2,1)S(1)}, bf16[4,512,192]{1,2,0:T(8,128)(2,1)}, u32[]{:S(2)}) copy-start(bf16[4,512,192]{1,2,0:T(8,128)(2,1)} %copy-done.19) | copy-start | bytes 2359300
  213.6 5.9 %copy-start.29 = (bf16[768,512]{1,0:T(8,128)(2,1)S(1)}, bf16[768,512]{1,0:T(8,128)(2,1)}, u32[]{:S(2)}) copy-start(bf16[768,512]{1,0:T(8,128)(2,1)} %copy.147) | copy-start | bytes 2359300
  214.5 13.0 %all-to-all-start.4 = ((bf16[4,128,576]{1,2,0:T(8,128)(2,1)}), bf16[4,128,576]{1,2,0:T(8,128)(2,1)S(1)}, u32[]{:S(2)}, u32[]{:S(2)}) async-start(bf16[4,128,576]{1,2,0:T(8,128)(2,1)} %copy.145), calls=%async_computation.4 | async-start | bytes 1179648 | tf_op jit(solution)/shard_map/all_to_all | solution.py:306
  231.2 6.8 %copy-start.22 = (bf16[2,32,10,768]{3,0,2,1:T(2,128)(2,1)S(1)}, bf16[2,32,10,768]{3,0,2,1:T(2,128)(2,1)}, u32[]{:S(2)}) copy-start(bf16[2,32,10,768]{3,0,2,1:T(2,128)(2,1)} %copy.138) | copy-start | bytes 2949124
  233.8 35.0 %all-to-all-start.5 = ((bf16[8,97,768]{2,1,0:T(8,128)(2,1)}), bf16[8,97,768]{2,1,0:T(8,128)(2,1)}, u32[]{:S(2)}, u32[]{:S(2)}) async-start(bf16[8,97,768]{2,1,0:T(8,128)(2,1)} %pad_maximum_fusion.1), calls=%async_computation.5 | async-start | bytes 2555904 | tf_op jit(solution)/shard_map/all_to_all | solution.py:340
  238.0 5.0 %copy-start.14 = (bf16[2,320,768]{2,0,1:T(2,128)(2,1)S(1)}, bf16[2,320,768]{2,0,1:T(2,128)(2,1)}, u32[]{:S(2)}) copy-start(bf16[2,320,768]{2,0,1:T(2,128)(2,1)} %copy-done.13) | copy-start | bytes 2949124
  238.0 5.0 %copy-start.28 = (bf16[2,320,768]{2,1,0:T(8,128)(2,1)S(1)}, bf16[2,320,768]{2,1,0:T(8,128)(2,1)}, u32[]{:S(2)}) copy-start(bf16[2,320,768]{2,1,0:T(8,128)(2,1)} %copy-done.27) | copy-start | bytes 2949124
  243.0 3.7 %copy-start.12 = (f32[128,768]{1,0:T(8,128)S(1)}, f32[128,768]{1,0:T(8,128)}, u32[]{:S(2)}) copy-start(f32[128,768]{1,0:T(8,128)} %copy-done.10) | copy-start | bytes 1179652
  243.0 3.7 %copy-start.16 = (f32[128,1536]{1,0:T(8,128)S(1)}, f32[128,1536]{1,0:T(8,128)}, u32[]{:S(2)}) copy-start(f32[128,1536]{1,0:T(8,128)} %copy-done.15) | copy-start | bytes 2359300
  243.0 3.7 %copy-start.25 = (bf16[1,128,768]{2,1,0:T(8,128)(2,1)S(1)}, bf16[1,128,768]{2,1,0:T(8,128)(2,1)}, u32[]{:S(2)}) copy-start(bf16[1,128,768]{2,1,0:T(8,128)(2,1)} %param.25) | copy-start | bytes 589828
  282.0 5.2 %copy-start.1 = (bf16[2,768,768]{2,1,0:T(8,128)(2,1)S(1)}, bf16[2,768,768]{2,1,0:T(8,128)(2,1)}, u32[]{:S(2)}) copy-start(bf16[2,768,768]{2,1,0:T(8,128)(2,1)} %param.23) | copy-start | bytes 7077892
Sparse Core Ops, SparseCore 0:
  10.2 20.8 all-gather.4
  89.3 19.3 all-gather.6

commit v2 on v1

--- a/solution.py
+++ b/solution.py
@@ -170,7 +170,7 @@
         out_specs=head_spec(buckets, total),
         out_shape=jax.ShapeDtypeStruct((heads, buckets, total), f32),
         cost_estimate=pl.CostEstimate(
-            flops=64 * heads * total * total,
+            flops=12000 * heads * total * total,
             bytes_accessed=4 * heads * total * total,
             transcendentals=0,
         ),
@@ -220,8 +220,10 @@
 
     def send_rows(rows):
         spread = dot(chosen, rows).astype(bf16).reshape(expert_ranks, local_slots, -1)
-        arrived = lax.all_to_all(spread, "experts", split_axis=0, concat_axis=0, tiled=True)
-        return lax.all_gather(arrived, "context", axis=0, tiled=True)
+        return lax.all_to_all(spread, "experts", split_axis=0, concat_axis=0, tiled=True)
+
+    def share_rows(rows):
+        return lax.all_gather(rows, "context", axis=0, tiled=True)
 
     shared = lax.all_gather(
         jnp.concatenate([block_input[0], bucket_ids.astype(bf16)], axis=1),
@@ -229,9 +231,11 @@
         axis=0,
         tiled=True,
     )
+    arrived_grads = send_rows((gates * grad_top).astype(bf16))
+    shared, arrived_grads = lax.optimization_barrier((shared, arrived_grads))
+    grad_rows = share_rows(arrived_grads)
     all_features = shared[:, :width].astype(f32)
     ids = shared[:, width:]
-    grad_rows = send_rows((gates * grad_top).astype(bf16))
     normed = rms_scale(all_features, first_gain).astype(bf16)
     weight = jnp.pad(
         qkv_weight.reshape(width, 3, heads * size), ((0, 0), (0, 0), (0, spare * size))
@@ -258,17 +262,24 @@
     high_wide = lax.reduce_precision(second_normed, 8, 7)
     high = high_wide.astype(bf16)
     low = (second_normed - high_wide).astype(bf16)
-    gathered = send_rows(jnp.concatenate([high, low], axis=1))
+    gathered = share_rows(send_rows(jnp.concatenate([high, low], axis=1)))
+
+    blocks = ranks * expert_ranks
+    many = blocks * local_slots
+    number = jnp.arange(many, dtype=jnp.int32)
+    source = number % (blocks * capacity)
+    source = (source // capacity) * local_slots + (
+        number // (blocks * capacity) * capacity + source % capacity
+    )
+    order = (source[:, None] == number[None, :]).astype(bf16)
 
     def by_expert(rows):
-        rows = rows.reshape(ranks * expert_ranks, experts_local, capacity, -1)
-        return rows.transpose(1, 0, 2, 3).reshape(
-            experts_local, ranks * expert_ranks * capacity, -1
-        )
+        moved = dot(order, rows.reshape(many, -1)).astype(bf16)
+        return moved.reshape(experts_local, blocks * capacity, -1)
 
     def by_block(rows):
-        rows = rows.reshape(experts_local, ranks, expert_ranks, capacity, -1)
-        return rows.transpose(1, 2, 0, 3, 4).reshape(ranks, expert_ranks, local_slots, -1)
+        moved = dot(order, rows.reshape(many, -1), TN).astype(bf16)
+        return moved.reshape(ranks // 2, 2, expert_ranks, local_slots, -1)
 
     wide = by_expert(gathered)
     grads = by_expert(grad_rows)
@@ -283,8 +294,17 @@
     forward_out = batched("xnf,xfd->xnd", hidden, expert_down).astype(bf16)
     back_in = batched("xnf,xdf->xnd", pre_grad, expert_in).astype(bf16)
     partial = by_block(jnp.concatenate([forward_out, back_in], axis=2))
-    pieces = lax.all_to_all(partial, "context", split_axis=0, concat_axis=0, tiled=True)
-    summed = jnp.sum(pieces.astype(f32), axis=0).astype(bf16)
+    pair, chip, chips = me % 2, me // 2, ranks // 2
+    held = lax.dynamic_index_in_dim(partial, pair, 1, keepdims=False)
+    passed = lax.dynamic_index_in_dim(partial, 1 - pair, 1, keepdims=False)
+    met = lax.ppermute(passed, "context", [(r, r ^ 1) for r in range(ranks)])
+    both = held.astype(f32) + met.astype(f32)
+    summed = lax.dynamic_index_in_dim(both, chip, 0, keepdims=False)
+    for hop in range(1, chips):
+        leaving = lax.dynamic_index_in_dim(both, (chip + hop) % chips, 0, keepdims=False)
+        route = [(r, (r // 2 + hop) % chips * 2 + r % 2) for r in range(ranks)]
+        summed = summed + lax.ppermute(leaving.astype(bf16), "context", route).astype(f32)
+    summed = summed.astype(bf16)
     returned = lax.all_to_all(summed, "experts", split_axis=0, concat_axis=0, tiled=True)
     picked = dot(chosen, returned.reshape(slots, 2 * width), TN)
     inner_grad = batched("xnd,xnf->xdf", high_rows, pre_grad)

time: 296 us -> 290 us (0.980)
  blocking collectives: 95.4 us -> 59.4 us
  matrix products: 29.5 us -> 38.5 us
  starting transfers between devices: 12.2 us -> 20.6 us
  local copies, waits for them, and re-layouts: 52.7 us -> 58.5 us
  other arithmetic: 13.7 us -> 17 us
  waiting for transfers between devices: 54.5 us -> 57.8 us
    all_to_all x1 -> x0, blocking collectives: 26.8 us -> none  [body(): lax.all_to_all(partial, 'context', split_axis=0, concat_axis=0, tiled=True)]
    all_to_all x2 -> x1, blocking collectives: 35.8 us -> 22.6 us  [send_rows(): lax.all_to_all(spread, 'experts', split_axis=0, concat_axis=0, tiled=True)]
    ppermute x0 -> x2, waiting for transfers between devices: none -> 13.2 us  [the longest x1 10.5 us: body(): lax.ppermute(leaving.astype(bf16), 'context', route).astype(f32)]
    all_gather x1, waiting for transfers between devices: 13.2 us -> 1.47 us  [body(): lax.all_gather(jnp.concatenate([block_input[0], bucket_ids.astype(bf16)],...]
    dot_general x9 -> x12, matrix products: 16 us -> 25.1 us  [dot(): return lax.dot_general(a, b, dims, preferred_element_type=f32)]
    reshape x0 -> x3, local copies, waits for them, and re-layouts: none -> 8.5 us  [the longest x2 6.05 us: by_expert(): moved = dot(order, rows.reshape(many, -1)).astype(bf16)]
    all_to_all x0 -> x1, starting transfers between devices: none -> 7.28 us  [send_rows(): lax.all_to_all(spread, 'experts', split_axis=0, concat_axis=0, tiled=True)]
    transpose x3 -> x0, local copies, waits for them, and re-layouts: 5.86 us -> none  [the longest x2 5.52 us: by_expert(): rows.transpose(1, 0, 2, 3)]
  transfers between devices with their start and end apart: 5 -> 8, of which waited for: 4 -> 8; matrix products, arithmetic and copies ran while one was open for 9% -> 12% of each run, Pallas kernels for 0% -> 0%
where the time goes in v2:
time: 290 us; the launch traced here: 288 us
  blocking collectives  59.4 us (20%)
  local copies, waits for them, and re-layouts  58.5 us (20%)
  waiting for transfers between devices  57.8 us (20%)
  matrix products  38.5 us (13%)
  Pallas kernels  21.5 us (7%)
  starting transfers between devices  20.6 us (7%)
  other arithmetic  17 us (6%)
  between operations  14.8 us (5%)
    dot_general x12, matrix products, dot(): return lax.dot_general(a, b, dims, preferred_element_type=f32)  25.1 us
    all_to_all x1, blocking collectives, send_rows(): lax.all_to_all(spread, 'experts', split_axis=0, concat_axis=0, tiled=True)  22.6 us
    all_to_all x1, waiting for transfers between devices, body(): lax.all_to_all(wide_part, 'experts', split_axis=0, concat_axis=0, tiled=T...  21 us
    unnamed x81, local copies, waits for them, and re-layouts  13.8 us
    all_to_all x1, waiting for transfers between devices, body(): lax.all_to_all(summed, 'experts', split_axis=0, concat_axis=0, tiled=True)  12.7 us
    all_gather x1, blocking collectives, share_rows(): return lax.all_gather(rows, 'context', axis=0, tiled=True)  12.4 us
    ppermute x1, waiting for transfers between devices, body(): lax.ppermute(leaving.astype(bf16), 'context', route).astype(f32)  10.5 us
    all_gather x1, blocking collectives, body(): lax.all_gather(att.transpose(1, 0, 2).reshape(total, share), 'context', a...  8.94 us
  transfers between devices with their start and end apart: 8, of which 8 were waited for; matrix products, arithmetic and copies ran while one was open for 12% of the time, Pallas kernels for 0%

profile of v2, /device:TPU:0, one launch (start us, length us, event | category | flops | bytes accessed | tf_op | source)
XLA Modules:
  0.0 288.0 jit_solution(13051661104823668625)
XLA Ops:
  8.4 1.7 pad_maximum_fusion.2
  12.7 7.3 %all-to-all-start = ((bf16[8,20,768]{2,1,0:T(8,128)(2,1)}), bf16[8,20,768]{2,1,0:T(8,128)(2,1)S(1)}, u32[]{:S(2)}, u32[]{:S(2)}) async-start(bf16[8,20,768]{2,1,0:T(8,128)(2,1)} %reshape.184), calls=%async_computation | async-start | bytes 589824 | tf_op jit(solution)/shard_map/all_to_all | solution.py:223
  20.1 5.8 %copy.102 = bf16[768,2304]{0,1:T(8,128)(2,1)} copy(bf16[768,2304]{1,0:T(8,128)(2,1)} %param.16) | data formatting | bytes 7077888 | tf_op args[3]
  27.2 2.5 all-to-all-done
  29.6 1.5 all-gather.5.cloned.1.call-done
  32.5 1.9 slice.49.ids_ref
  34.4 2.7 convolution_convert_fusion.6
  37.1 2.3 copy.103
  40.8 7.0 %attend.1 = (bf16[3,512,64]{2,1,0:T(8,128)(2,1)S(1)}, bf16[3,512,512]{2,1,0:T(8,128)(2,1)S(1)}) custom-call(bf16[3,512,64]{2,1,0:T(8,128)(2,1)S(1)} %get-tuple-element.35.q_ref, bf16[3,512,64]{2,1,0:T(8,128)(2,1)S(1)} %get-tuple-element.34.k_ref, bf16[3,512,64]{2,1,0:T(8,128)(2,1)S(1)} %get-tuple-element.33.v_ref, ...), custom_call_target="tpu_custom_call" | custom-call | flops 201326592 | bytes 3145728 | tf_op jit(solution)/shard_map/attend/pallas_call | solution.py:123
  49.6 1.8 copy.104
  51.5 8.9 %all_gather.22 = bf16[4,512,192]{1,2,0:T(8,128)(2,1)S(1)} all-gather(bf16[1,512,192]{1,2,0:T(8,128)(2,1)} %bitcast.141), channel_id=1, replica_groups=mesh['experts'=8,'context'=4] {'context'}, dimensions={0}, use_global_device_ids=true | all-gather | bytes 983040 | tf_op jit(solution)/shard_map/all_gather | solution.py:254
  60.4 2.0 multiply_reduce_fusion.2
  64.4 1.9 reshape.189
  66.4 22.6 %all_to_all.25 = bf16[8,20,1536]{2,1,0:T(8,128)(2,1)S(1)} all-to-all(bf16[8,20,1536]{2,1,0:T(8,128)(2,1)} %reshape.189), channel_id=1, replica_groups=mesh['experts'=8,'context'=4] {'experts'}, dimensions={0} | all-to-all | bytes 983040 | tf_op jit(solution)/shard_map/all_to_all | solution.py:223
  91.5 12.4 %all_gather.24 = bf16[32,20,768]{2,0,1:T(8,128)(2,1)S(1)} all-gather(bf16[8,20,768]{2,0,1:T(8,128)(2,1)S(1)} %copy.107), channel_id=1, replica_groups=mesh['experts'=8,'context'=4] {'context'}, dimensions={0}, use_global_device_ids=true | all-gather | bytes 1228800 | tf_op jit(solution)/shard_map/all_gather | solution.py:226
  103.9 1.6 copy.108
  105.5 2.1 reshape.192
  107.6 3.2 %fusion.4 = bf16[640,768]{1,0:T(8,128)(2,1)} fusion(bf16[640,768]{1,0:T(8,128)(2,1)} %reshape.192, s32[640]{0:T(1024)} %fusion.58), kind=kOutput, calls=%fused_computation.18 | convolution fusion | flops 630046720 | bytes 1968640 | tf_op jit(solution)/shard_map/dot_general | solution.py:25
  111.4 4.0 %copy.106 = bf16[32,20,1536]{2,1,0:T(8,128)(2,1)} copy(bf16[32,20,1536]{2,0,1:T(8,128)(2,1)} %all-gather.7.cloned.1.call-done) | data formatting | bytes 3932160 | tf_op jit(solution)/shard_map/all_gather | solution.py:226
  115.4 3.9 %reshape.190 = bf16[640,1536]{1,0:T(8,128)(2,1)} reshape(bf16[32,20,1536]{2,1,0:T(8,128)(2,1)} %copy.106) | data formatting | bytes 3932160 | tf_op jit(solution)/shard_map/reshape | solution.py:277
  119.4 3.3 %convolution_convert_fusion.1 = bf16[640,1536]{1,0:T(8,128)(2,1)S(1)} fusion(bf16[640,1536]{1,0:T(8,128)(2,1)} %reshape.190, s32[640]{0:T(1024)} %fusion.58), kind=kOutput, calls=%fused_computation.1 | convolution fusion | flops 1259683840 | bytes 3934720 | tf_op jit(solution)/shard_map/dot_general | solution.py:25
  129.6 3.1 %convolution_convert_fusion = bf16[640,1536]{1,0:T(8,128)(2,1)} fusion(bf16[640,1536]{1,0:T(8,128)(2,1)S(1)} %bitcast.134, s32[640]{0:T(1024)S(1)} %copy-done.35), kind=kOutput, calls=%fused_computation | convolution fusion | flops 1259683840 | bytes 3934720 | tf_op jit(solution)/shard_map/dot_general | solution.py:25
  132.7 2.5 reshape.195
  136.7 2.7 collective-permute-done
  139.4 1.6 convert_add_fusion
  142.6 1.5 collective-permute-start.1
  145.5 10.5 %collective-permute-done.1 = bf16[8,20,1536]{2,0,1:T(8,128)(2,1)S(1)} collective-permute-done((bf16[8,20,1536]{2,0,1:T(8,128)(2,1)S(1)}, bf16[8,20,1536]{2,0,1:T(8,128)(2,1)S(1)}, u32[]{:S(2)}, u32[]{:S(2)}) %collective-permute-start.1) | collective-permute-done | bytes 491552 | tf_op jit(solution)/shard_map/ppermute | solution.py:306
  157.6 3.8 %all-to-all-start.2 = ((bf16[8,20,1536]{2,1,0:T(8,128)(2,1)}), bf16[8,20,1536]{2,1,0:T(8,128)(2,1)S(1)}, u32[]{:S(2)}, u32[]{:S(2)}) async-start(bf16[8,20,1536]{2,1,0:T(8,128)(2,1)} %copy.113), calls=%async_computation.2 | async-start | bytes 1179648 | tf_op jit(solution)/shard_map/all_to_all | solution.py:308
  164.1 12.7 %all-to-all-done.2 = bf16[8,20,1536]{2,1,0:T(8,128)(2,1)S(1)} async-done(((bf16[8,20,1536]{2,1,0:T(8,128)(2,1)}), bf16[8,20,1536]{2,1,0:T(8,128)(2,1)S(1)}, u32[]{:S(2)}, u32[]{:S(2)}) %all-to-all-start.2) | async-done | bytes 491552 | tf_op jit(solution)/shard_map/all_to_all | solution.py:308
  178.6 8.6 %all_gather.25 = bf16[512,768]{1,0:T(8,128)(2,1)S(1)} all-gather(bf16[128,768]{1,0:T(8,128)(2,1)S(1)} %fusion.77), channel_id=1, replica_groups=mesh['experts'=8,'context'=4] {'context'}, dimensions={0}, use_global_device_ids=true | all-gather | bytes 983040 | tf_op jit(solution)/shard_map/all_gather | solution.py:317
  187.2 1.6 convolution_convert_fusion.9
  191.7 6.7 %attend_back.1 = (bf16[3,512,64]{2,1,0:T(8,128)(2,1)S(1)}, bf16[3,512,64]{2,1,0:T(8,128)(2,1)S(1)}, bf16[3,512,64]{2,1,0:T(8,128)(2,1)S(1)}, bf16[3,512,512]{2,1,0:T(8,128)(2,1)S(1)}) custom-call(bf16[3,512,64]{2,1,0:T(8,128)(2,1)S(1)} %get-tuple-element.35.q_ref, bf16[3,512,64]{2,1,0:T(8,128)(2,1)S(1)} %get-tuple-element.34.k_ref, ...), custom_call_target="tpu_custom_call" | custom-call | flops 402653184 | bytes 6291456 | tf_op jit(solution)/shard_map/attend_back/pallas_call | solution.py:147
  198.4 7.8 %table_sums.1 = f32[3,32,512]{2,1,0:T(8,128)S(1)} custom-call(bf16[3,512,512]{2,1,0:T(8,128)(2,1)S(1)} %get-tuple-element.24.ds_ref, bf16[512,512]{1,0:T(8,128)(2,1)S(1)} %copy-done.3), custom_call_target="tpu_custom_call" | custom-call | flops 9437184000 | bytes 3145728 | tf_op jit(solution)/shard_map/table_sums/pallas_call | solution.py:166
  208.5 3.5 %all-to-all-start.3 = ((bf16[4,128,576]{1,2,0:T(8,128)(2,1)}), bf16[4,128,576]{1,2,0:T(8,128)(2,1)S(1)}, u32[]{:S(2)}, u32[]{:S(2)}) async-start(bf16[4,128,576]{1,2,0:T(8,128)(2,1)} %copy.116), calls=%async_computation.3 | async-start | bytes 1179648 | tf_op jit(solution)/shard_map/all_to_all | solution.py:326
  211.9 1.5 convolution_convert_fusion.7
  213.5 1.8 convolution_convert_fusion.3
  215.2 6.2 %all-to-all-done.3 = bf16[4,128,576]{1,2,0:T(8,128)(2,1)S(1)} async-done(((bf16[4,128,576]{1,2,0:T(8,128)(2,1)}), bf16[4,128,576]{1,2,0:T(8,128)(2,1)S(1)}, u32[]{:S(2)}, u32[]{:S(2)}) %all-to-all-start.3) | async-done | bytes 589856 | tf_op jit(solution)/shard_map/all_to_all | solution.py:326
  221.5 3.4 %fusion.23 = (bf16[768]{0:T(1024)(128)(2,1)S(1)}, f32[128]{0:T(128)S(1)}, f32[128,768]{1,0:T(8,128)S(1)}) fusion(f32[128]{0:T(128)S(1)} %fusion.73, bf16[1,128,768]{2,1,0:T(8,128)(2,1)S(1)} %copy-done.15, f32[768]{0:T(1024)S(1)} %copy-done.30, bf16[128,2304]{0,1:T(8,128)(2,1)S(1)} %bitcast.130, bf16[768,2304]{1,0:T(8,128)(2,1)} %param.16), kind=kOutput, calls=%fused_computation.60 | convolution fusion | flops 453672064 | bytes 4724224 | tf_op jit(solution)/shard_map/dot_general | solution.py:25
  225.1 2.6 pad_maximum_fusion.1
  227.7 4.3 %all-to-all-start.4 = ((bf16[8,97,768]{2,1,0:T(8,128)(2,1)}), bf16[8,97,768]{2,1,0:T(8,128)(2,1)}, u32[]{:S(2)}, u32[]{:S(2)}) async-start(bf16[8,97,768]{2,1,0:T(8,128)(2,1)} %pad_maximum_fusion.1), calls=%async_computation.4 | async-start | bytes 2555904 | tf_op jit(solution)/shard_map/all_to_all | solution.py:360
  232.0 5.0 %fusion.7 = f32[2,768,768]{2,1,0:T(8,128)} fusion(bf16[2,320,768]{2,1,0:T(8,128)(2,1)S(1)} %copy-done.27, bf16[2,320,1536]{2,1,0:T(8,128)(2,1)} %bitcast.133), kind=kOutput, calls=%fused_computation.34 | convolution fusion | flops 754974720 | bytes 6684672 | tf_op jit(solution)/shard_map/xnd,xnf->xdf/dot_general | solution.py:310
  237.0 3.6 %fusion.29 = f32[2,768,768]{2,1,0:T(8,128)} fusion(bf16[2,320,768]{2,1,0:T(8,128)(2,1)S(1)} %bitcast.137, bf16[2,320,768]{2,1,0:T(8,128)(2,1)S(1)} %copy-done.25), kind=kOutput, calls=%fused_computation.73 | convolution fusion | flops 756449280 | bytes 6684672 | tf_op jit(solution)/shard_map/xnf,xnd->xfd/dot_general | solution.py:311
  241.7 21.0 %all-to-all-done.4 = bf16[8,97,768]{2,1,0:T(8,128)(2,1)} async-done(((bf16[8,97,768]{2,1,0:T(8,128)(2,1)}), bf16[8,97,768]{2,1,0:T(8,128)(2,1)}, u32[]{:S(2)}, u32[]{:S(2)}) %all-to-all-start.4) | async-done | bytes 1191968 | tf_op jit(solution)/shard_map/all_to_all | solution.py:360
  262.7 1.5 reduce_sum.130
  264.2 6.9 %all-gather.1 = bf16[4,97,768]{2,1,0:T(8,128)(2,1)S(1)} all-gather(bf16[1,97,768]{2,1,0:T(8,128)(2,1)S(1)} %bitcast.142), channel_id=2, replica_groups=mesh['experts'=8,'context'=4] {'context'}, dimensions={0}, use_global_device_ids=true | all-gather | bytes 744960 | tf_op jit(solution)/shard_map/all_gather | solution.py:362
  274.1 1.9 copy.129
  276.0 1.5 copy.124
  277.5 2.9 %reshape_reshape.11 = f32[96,2304]{1,0:T(8,128)} reshape(f32[96,3,4,192]{3,2,1,0:T(4,128)} %copy.124) | data formatting | bytes 1769472 | tf_op jit(solution)/shard_map/reshape;reshape | solution.py:365
  (149 shorter events, 42.4 us)
Async XLA Ops:
  7.2 115.5 %copy-start = (bf16[2,768,768]{2,1,0:T(8,128)(2,1)S(1)}, bf16[2,768,768]{2,1,0:T(8,128)(2,1)}, u32[]{:S(2)}) copy-start(bf16[2,768,768]{2,1,0:T(8,128)(2,1)} %param.23) | copy-start | bytes 7077892
  7.2 12.9 %copy-start.31 = (f32[32,12]{0,1:T(8,128)S(1)}, f32[32,12]{0,1:T(8,128)}, u32[]{:S(2)}) copy-start(f32[32,12]{0,1:T(8,128)} %param.18) | copy-start | bytes 4612
  7.2 23.9 %all-gather.5.cloned.1.call-start = ((), (), s32[]{:S(2)}) async-start(), calls=%async_computation.5 | async-start | bytes 1638400 | tf_op jit(solution)/shard_map/all_gather | solution.py:228
  10.7 2.0 copy-start.32
  12.7 16.9 %all-to-all-start = ((bf16[8,20,768]{2,1,0:T(8,128)(2,1)}), bf16[8,20,768]{2,1,0:T(8,128)(2,1)S(1)}, u32[]{:S(2)}, u32[]{:S(2)}) async-start(bf16[8,20,768]{2,1,0:T(8,128)(2,1)} %reshape.184), calls=%async_computation | async-start | bytes 589824 | tf_op jit(solution)/shard_map/all_to_all | solution.py:223
  20.0 91.4 %all-gather.7.cloned.1.call-start = ((), (), s32[]{:S(2)}) async-start(), calls=%async_computation.6 | async-start | bytes 2457600 | tf_op jit(solution)/shard_map/all_gather | solution.py:226
  25.9 8.5 %copy-start.30 = (f32[768]{0:T(1024)S(1)}, f32[768]{0:T(1024)}, u32[]{:S(2)}) copy-start(f32[768]{0:T(1024)} %param.14) | copy-start | bytes 9220
  29.6 7.4 %copy-start.21 = (bf16[8,20,768]{2,1,0:T(8,128)(2,1)}, bf16[8,20,768]{2,1,0:T(8,128)(2,1)S(1)}, u32[]{:S(2)}) copy-start(bf16[8,20,768]{2,1,0:T(8,128)(2,1)S(1)} %all-to-all-done) | copy-start | bytes 737284
  39.4 1.4 copy-start.2
  47.7 1.1 copy-start.4
  48.9 0.7 copy-start.5
  49.6 13.6 %copy-start.29 = (f32[768]{0:T(1024)S(1)}, f32[768]{0:T(1024)}, u32[]{:S(2)}) copy-start(f32[768]{0:T(1024)} %param.15) | copy-start | bytes 9220
  51.5 11.9 %copy-start.33 = (s32[128]{0:T(128)S(1)}, s32[128]{0:T(128)}, u32[]{:S(2)}) copy-start(s32[128]{0:T(128)} %copy-done.32) | copy-start | bytes 1540
  60.4 2.9 %copy-start.17 = (bf16[4,512,192]{1,2,0:T(8,128)(2,1)}, bf16[4,512,192]{1,2,0:T(8,128)(2,1)S(1)}, u32[]{:S(2)}) copy-start(bf16[4,512,192]{1,2,0:T(8,128)(2,1)S(1)} %all_gather.22) | copy-start | bytes 2359300
  62.4 0.5 copy-start.37
  62.4 0.8 copy-start.8
  122.7 1.3 copy-start.19
  124.0 1.2 copy-start.22
  124.0 2.0 copy-start.39
  125.0 2.9 %copy-start.24 = (bf16[2,320,768]{2,1,0:T(8,128)(2,1)}, bf16[2,320,768]{2,1,0:T(8,128)(2,1)S(1)}, u32[]{:S(2)}) copy-start(bf16[2,320,768]{2,1,0:T(8,128)(2,1)S(1)} %get-tuple-element.41) | copy-start | bytes 2949124
  127.0 1.0 copy-start.26
  128.9 0.7 copy-start.35
  136.5 2.9 %collective-permute-start = (bf16[2,8,20,1536]{3,1,2,0:T(8,128)(2,1)}, bf16[2,8,20,1536]{3,1,2,0:T(8,128)(2,1)}, u32[]{:S(2)}, u32[]{:S(2)}) collective-permute-start(bf16[2,8,20,1536]{3,1,2,0:T(8,128)(2,1)} %bitcast.116), channel_id=1, source_target_pairs={{0,1},{1,0},{2,3},{3,2},{4,5},{5,4},{6,7},{7,6},{8,9},{9,8},{10,11... | collective-permute-start | bytes 2949128 | tf_op jit(solution)/shard_map/ppermute | solution.py:300
  141.0 1.4 copy-start.11
  142.6 13.4 %collective-permute-start.1 = (bf16[8,20,1536]{2,0,1:T(8,128)(2,1)S(1)}, bf16[8,20,1536]{2,0,1:T(8,128)(2,1)S(1)}, u32[]{:S(2)}, u32[]{:S(2)}) collective-permute-start(bf16[8,20,1536]{2,0,1:T(8,128)(2,1)S(1)} %copy.112), channel_id=1, source_target_pairs={{0,2},{1,3},{2,0},{3,1},{4,6},{5,7},{6,4},{7,5},{8,10},{9,11},{10,... | collective-permute-start | bytes 1474568 | tf_op jit(solution)/shard_map/ppermute | solution.py:306
  145.5 15.8 %copy-start.14 = (bf16[1,128,768]{2,1,0:T(8,128)(2,1)S(1)}, bf16[1,128,768]{2,1,0:T(8,128)(2,1)}, u32[]{:S(2)}) copy-start(bf16[1,128,768]{2,1,0:T(8,128)(2,1)} %param.13) | copy-start | bytes 589828
  157.6 19.2 %all-to-all-start.2 = ((bf16[8,20,1536]{2,1,0:T(8,128)(2,1)}), bf16[8,20,1536]{2,1,0:T(8,128)(2,1)S(1)}, u32[]{:S(2)}, u32[]{:S(2)}) async-start(bf16[8,20,1536]{2,1,0:T(8,128)(2,1)} %copy.113), calls=%async_computation.2 | async-start | bytes 1179648 | tf_op jit(solution)/shard_map/all_to_all | solution.py:308
  161.5 15.4 %copy-start.34 = (s32[128]{0:T(128)S(1)}, s32[128]{0:T(128)}, u32[]{:S(2)}) copy-start(s32[128]{0:T(128)} %copy-done.32) | copy-start | bytes 1540
  162.9 14.3 %copy-start.9 = (f32[128,768]{1,0:T(8,128)S(1)}, f32[128,768]{1,0:T(8,128)}, u32[]{:S(2)}) copy-start(f32[128,768]{1,0:T(8,128)} %copy-done.8) | copy-start | bytes 1179652
  164.1 13.3 %copy-start.38 = (f32[128]{0:T(128)S(1)}, f32[128]{0:T(128)}, u32[]{:S(2)}) copy-start(f32[128]{0:T(128)} %copy-done.37) | copy-start | bytes 1540
  177.3 11.5 %copy-start.12 = (f32[128,1536]{1,0:T(8,128)}, f32[128,1536]{1,0:T(8,128)S(1)}, u32[]{:S(2)}) copy-start(f32[128,1536]{1,0:T(8,128)S(1)} %fusion.40) | copy-start | bytes 2359300
  187.2 1.6 copy-start.16
  188.8 9.6 %copy-start.3 = (bf16[512,512]{1,0:T(8,128)(2,1)S(1)}, bf16[512,512]{1,0:T(8,128)(2,1)}, u32[]{:S(2)}) copy-start(bf16[512,512]{1,0:T(8,128)(2,1)} %slice.49.ids_ref) | copy-start | bytes 1572868
  189.7 1.0 copy-start.6
  190.7 1.0 copy-start.7
  207.1 4.8 %copy-start.18 = (bf16[4,512,192]{1,2,0:T(8,128)(2,1)S(1)}, bf16[4,512,192]{1,2,0:T(8,128)(2,1)}, u32[]{:S(2)}) copy-start(bf16[4,512,192]{1,2,0:T(8,128)(2,1)} %copy-done.17) | copy-start | bytes 2359300
  207.6 5.9 %copy-start.28 = (bf16[768,512]{1,0:T(8,128)(2,1)S(1)}, bf16[768,512]{1,0:T(8,128)(2,1)}, u32[]{:S(2)}) copy-start(bf16[768,512]{1,0:T(8,128)(2,1)} %copy.118) | copy-start | bytes 2359300
  208.5 13.0 %all-to-all-start.3 = ((bf16[4,128,576]{1,2,0:T(8,128)(2,1)}), bf16[4,128,576]{1,2,0:T(8,128)(2,1)S(1)}, u32[]{:S(2)}, u32[]{:S(2)}) async-start(bf16[4,128,576]{1,2,0:T(8,128)(2,1)} %copy.116), calls=%async_computation.3 | async-start | bytes 1179648 | tf_op jit(solution)/shard_map/all_to_all | solution.py:326
  213.4 8.1 %copy-start.15 = (bf16[1,128,768]{2,1,0:T(8,128)(2,1)S(1)}, bf16[1,128,768]{2,1,0:T(8,128)(2,1)}, u32[]{:S(2)}) copy-start(bf16[1,128,768]{2,1,0:T(8,128)(2,1)} %param.13) | copy-start | bytes 589828
  225.1 6.8 %copy-start.27 = (bf16[2,320,768]{2,1,0:T(8,128)(2,1)S(1)}, bf16[2,320,768]{2,1,0:T(8,128)(2,1)}, u32[]{:S(2)}) copy-start(bf16[2,320,768]{2,1,0:T(8,128)(2,1)} %copy-done.26) | copy-start | bytes 2949124
  227.7 35.0 %all-to-all-start.4 = ((bf16[8,97,768]{2,1,0:T(8,128)(2,1)}), bf16[8,97,768]{2,1,0:T(8,128)(2,1)}, u32[]{:S(2)}, u32[]{:S(2)}) async-start(bf16[8,97,768]{2,1,0:T(8,128)(2,1)} %pad_maximum_fusion.1), calls=%async_computation.4 | async-start | bytes 2555904 | tf_op jit(solution)/shard_map/all_to_all | solution.py:360
  232.0 5.0 %copy-start.23 = (bf16[640,768]{1,0:T(8,128)(2,1)S(1)}, bf16[640,768]{1,0:T(8,128)(2,1)}, u32[]{:S(2)}) copy-start(bf16[640,768]{1,0:T(8,128)(2,1)} %fusion.4) | copy-start | bytes 2949124
  232.0 5.0 %copy-start.25 = (bf16[2,320,768]{2,1,0:T(8,128)(2,1)S(1)}, bf16[2,320,768]{2,1,0:T(8,128)(2,1)}, u32[]{:S(2)}) copy-start(bf16[2,320,768]{2,1,0:T(8,128)(2,1)} %copy-done.24) | copy-start | bytes 2949124
  236.9 3.7 %copy-start.10 = (f32[128,768]{1,0:T(8,128)S(1)}, f32[128,768]{1,0:T(8,128)}, u32[]{:S(2)}) copy-start(f32[128,768]{1,0:T(8,128)} %copy-done.8) | copy-start | bytes 1179652
  237.0 3.7 %copy-start.13 = (f32[128,1536]{1,0:T(8,128)S(1)}, f32[128,1536]{1,0:T(8,128)}, u32[]{:S(2)}) copy-start(f32[128,1536]{1,0:T(8,128)} %copy-done.12) | copy-start | bytes 2359300
  237.0 3.7 %copy-start.20 = (bf16[1,128,768]{2,1,0:T(8,128)(2,1)S(1)}, bf16[1,128,768]{2,1,0:T(8,128)(2,1)}, u32[]{:S(2)}) copy-start(bf16[1,128,768]{2,1,0:T(8,128)(2,1)} %param.25) | copy-start | bytes 589828
  237.0 3.7 %copy-start.36 = (f32[1,128]{1,0:T(1,128)S(1)}, f32[1,128]{1,0:T(1,128)}, u32[]{:S(2)}) copy-start(f32[1,128]{1,0:T(1,128)} %param.22) | copy-start | bytes 1540
  276.0 5.2 %copy-start.1 = (bf16[2,768,768]{2,1,0:T(8,128)(2,1)S(1)}, bf16[2,768,768]{2,1,0:T(8,128)(2,1)}, u32[]{:S(2)}) copy-start(bf16[2,768,768]{2,1,0:T(8,128)(2,1)} %param.23) | copy-start | bytes 7077892
Sparse Core Ops, SparseCore 0:
  10.2 20.8 all-gather.4
  90.0 21.3 all-gather.6

commit v3 on v2

--- a/solution.py
+++ b/solution.py
@@ -215,15 +215,17 @@
     features = block_input[0].astype(f32)
     gates = gate_value[0][:, None]
     grad_top = upstream[0].astype(f32)
-    place = expert_route[0] * capacity + expert_slot[0]
+    place = (expert_route[0] % experts_local) * capacity + expert_slot[0]
+    place = place * expert_ranks + expert_route[0] // experts_local
     chosen = (place[None, :] == jnp.arange(slots, dtype=jnp.int32)[:, None]).astype(bf16)
 
     def send_rows(rows):
-        spread = dot(chosen, rows).astype(bf16).reshape(expert_ranks, local_slots, -1)
-        return lax.all_to_all(spread, "experts", split_axis=0, concat_axis=0, tiled=True)
+        spread = dot(chosen, rows).astype(bf16).reshape(local_slots, expert_ranks, -1)
+        moved = lax.all_to_all(spread, "experts", split_axis=1, concat_axis=1, tiled=True)
+        return moved.reshape(slots, -1)
 
     def share_rows(rows):
-        return lax.all_gather(rows, "context", axis=0, tiled=True)
+        return lax.all_gather(rows, "context", axis=0, tiled=False)
 
     shared = lax.all_gather(
         jnp.concatenate([block_input[0], bucket_ids.astype(bf16)], axis=1),
@@ -264,22 +266,15 @@
     low = (second_normed - high_wide).astype(bf16)
     gathered = share_rows(send_rows(jnp.concatenate([high, low], axis=1)))
 
-    blocks = ranks * expert_ranks
-    many = blocks * local_slots
-    number = jnp.arange(many, dtype=jnp.int32)
-    source = number % (blocks * capacity)
-    source = (source // capacity) * local_slots + (
-        number // (blocks * capacity) * capacity + source % capacity
-    )
-    order = (source[:, None] == number[None, :]).astype(bf16)
+    per_expert = capacity * expert_ranks
 
     def by_expert(rows):
-        moved = dot(order, rows.reshape(many, -1)).astype(bf16)
-        return moved.reshape(experts_local, blocks * capacity, -1)
+        rows = rows.reshape(ranks, experts_local, per_expert, -1).transpose(1, 0, 2, 3)
+        return rows.reshape(experts_local, ranks * per_expert, -1)
 
     def by_block(rows):
-        moved = dot(order, rows.reshape(many, -1), TN).astype(bf16)
-        return moved.reshape(ranks // 2, 2, expert_ranks, local_slots, -1)
+        rows = rows.reshape(experts_local, ranks, per_expert, -1).transpose(1, 0, 2, 3)
+        return rows.reshape(ranks // 2, 2, slots, -1)
 
     wide = by_expert(gathered)
     grads = by_expert(grad_rows)
@@ -305,7 +300,13 @@
         route = [(r, (r // 2 + hop) % chips * 2 + r % 2) for r in range(ranks)]
         summed = summed + lax.ppermute(leaving.astype(bf16), "context", route).astype(f32)
     summed = summed.astype(bf16)
-    returned = lax.all_to_all(summed, "experts", split_axis=0, concat_axis=0, tiled=True)
+    returned = lax.all_to_all(
+        summed.reshape(local_slots, expert_ranks, 2 * width),
+        "experts",
+        split_axis=1,
+        concat_axis=1,
+        tiled=True,
+    )
     picked = dot(chosen, returned.reshape(slots, 2 * width), TN)
     inner_grad = batched("xnd,xnf->xdf", high_rows, pre_grad)
     down_grad = batched("xnf,xnd->xfd", hidden, grads)
@@ -323,23 +324,10 @@
     )
     dq, dk, dv, d_scores = attend_back(q, k, v, att, d_att, probs)
     d_qkv = jnp.stack([dq, dk, dv]).transpose(2, 0, 1, 3).reshape(total, 3 * share)
-    own = lax.all_to_all(
-        d_qkv.reshape(ranks, local_rows, 3 * share),
-        "context",
-        split_axis=0,
-        concat_axis=0,
-        tiled=True,
-    )
-    own = own.reshape(ranks, local_rows, 3, share).transpose(1, 2, 0, 3)
-    own = own.reshape(local_rows, 3, ranks * share)[:, :, :width].reshape(local_rows, 3 * width)
-    d_first = dot(own, qkv_weight, NT)
-    _, first_pull = jax.vjp(rms_scale, features, first_gain)
-    d_input_norm, first_part = first_pull(d_first)
-    input_grad = (d_middle + d_input_norm)[None]
-
     my_d_middle = lax.dynamic_slice_in_dim(all_d_middle, me * columns, columns, 1)
     qkv_part = dot(normed, d_qkv, TN)
     proj_part = dot(all_att, my_d_middle, TN)
+    d_scores, qkv_part = lax.optimization_barrier((d_scores, qkv_part))
     table_part = table_sums(d_scores, ids, buckets).T
     wide_part = jnp.concatenate([qkv_part, proj_part], axis=1).astype(bf16)
     grad_width = 3 * share + columns
@@ -347,7 +335,6 @@
     table_out = buckets // expert_ranks
     small = jnp.concatenate(
         [
-            first_part.reshape(expert_ranks, rows_out),
             second_part.reshape(expert_ranks, rows_out),
             table_part.reshape(expert_ranks, table_out * group),
         ],
@@ -358,16 +345,40 @@
         [wide_part.reshape(expert_ranks, rows_out, grad_width), small[:, None, :]], axis=1
     )
     sums = lax.all_to_all(wide_part, "experts", split_axis=0, concat_axis=0, tiled=True)
-    sums = jnp.sum(sums.astype(f32), axis=0).astype(bf16)
+    outgoing = d_qkv.reshape(ranks, local_rows, 3 * share)
+    own = lax.dynamic_update_index_in_dim(
+        jnp.zeros_like(outgoing), lax.dynamic_index_in_dim(outgoing, me, 0), me, 0
+    )
+    for hop in range(1, ranks):
+        leaving = lax.dynamic_index_in_dim(outgoing, (me + hop) % ranks, 0)
+        met = lax.ppermute(leaving, "context", [(r, (r + hop) % ranks) for r in range(ranks)])
+        own = lax.dynamic_update_index_in_dim(own, met, (me - hop) % ranks, 0)
+    own = own.reshape(ranks, local_rows, 3, share).transpose(1, 2, 0, 3)
+    own = own.reshape(local_rows, 3, ranks * share)[:, :, :width].reshape(local_rows, 3 * width)
+    d_first = dot(own, qkv_weight, NT)
+    _, first_pull = jax.vjp(rms_scale, features, first_gain)
+    d_input_norm, first_part = first_pull(d_first)
+    input_grad = (d_middle + d_input_norm)[None]
+
+    first_rows = lax.all_to_all(
+        first_part.astype(bf16).reshape(expert_ranks, 1, rows_out),
+        "experts",
+        split_axis=0,
+        concat_axis=0,
+        tiled=True,
+    )
+    first_sum = jnp.sum(first_rows.astype(f32), axis=0)
+    first_row = jnp.pad(first_sum, ((0, 0), (0, grad_width - rows_out)))
+    sums = jnp.concatenate([jnp.sum(sums.astype(f32), axis=0), first_row], axis=0).astype(bf16)
     full = lax.all_gather(sums, "context", axis=0, tiled=False).astype(f32)
     qkv_grad = full[:, :rows_out, : 3 * share].reshape(ranks, rows_out, 3, share)
     qkv_grad = qkv_grad.transpose(1, 2, 0, 3).reshape(rows_out, 3, ranks * share)
     qkv_grad = qkv_grad[:, :, :width].reshape(rows_out, 3 * width)
     proj_grad = full[:, :rows_out, 3 * share :].transpose(1, 0, 2).reshape(rows_out, width)
     last = full[:, rows_out]
-    first_grad = jnp.sum(last[:, :rows_out], axis=0)
-    second_grad = jnp.sum(last[:, rows_out : 2 * rows_out], axis=0)
-    table_grad = last[:, 2 * rows_out : 2 * rows_out + table_out * group]
+    first_grad = jnp.sum(full[:, rows_out + 1, :rows_out], axis=0)
+    second_grad = jnp.sum(last[:, :rows_out], axis=0)
+    table_grad = last[:, rows_out : rows_out + table_out * group]
     table_grad = table_grad.reshape(ranks, table_out, group).transpose(1, 0, 2)
     table_grad = table_grad.reshape(table_out, ranks * group)[:, :heads]
     return (

time: 290 us -> 285 us (0.983)
  waiting for transfers between devices: 57.8 us -> 78 us
  local copies, waits for them, and re-layouts: 58.5 us -> 44.2 us
  matrix products: 38.5 us -> 29.4 us
  starting transfers between devices: 20.6 us -> 24.3 us
    ppermute x0 -> x3, waiting for transfers between devices: none -> 11.5 us  [body(): lax.ppermute(leaving, 'context', [(r, (r + hop) % ranks) for r in range(r...]
    dot_general x12 -> x9, matrix products: 25.1 us -> 15.9 us  [dot(): return lax.dot_general(a, b, dims, preferred_element_type=f32)]
    all_gather x1, waiting for transfers between devices: 0.62 us -> 9.02 us  [share_rows(): return lax.all_gather(rows, 'context', axis=0, tiled=False)]
    reshape x7 -> x4, local copies, waits for them, and re-layouts: 11.4 us -> 3.3 us  [the longest x1 1.43 us: by_block(): rows.reshape(experts_local, ranks, per_expert, -1).transpose(1, 0, 2, 3)]
    all_gather x2 -> x0, local copies, waits for them, and re-layouts: 5.6 us -> none  [share_rows(): return lax.all_gather(rows, 'context', axis=0, tiled=True)]
    ppermute x0 -> x3, starting transfers between devices: none -> 2.99 us  [body(): lax.ppermute(leaving, 'context', [(r, (r + hop) % ranks) for r in range(r...]
    unnamed x81 -> x95, local copies, waits for them, and re-layouts: 13.8 us -> 11.1 us
  transfers between devices with their start and end apart: 8 -> 11, of which waited for: 8 -> 11; matrix products, arithmetic and copies ran while one was open for 12% -> 9% of each run, Pallas kernels for 0% -> 0%
where the time goes in v3:
time: 285 us; the launch traced here: 284 us
  waiting for transfers between devices  78 us (27%)
  blocking collectives  56.5 us (20%)
  local copies, waits for them, and re-layouts  44.2 us (16%)
  matrix products  29.4 us (10%)
  starting transfers between devices  24.3 us (9%)
  Pallas kernels  21.4 us (8%)
  other arithmetic  14.9 us (5%)
  between operations  14.8 us (5%)
    all_to_all x1, blocking collectives, send_rows(): lax.all_to_all(spread, 'experts', split_axis=1, concat_axis=1, tiled=True)  22.4 us
    all_to_all x1, waiting for transfers between devices, body(): lax.all_to_all(wide_part, 'experts', split_axis=0, concat_axis=0, tiled=T...  21.1 us
    dot_general x9, matrix products, dot(): return lax.dot_general(a, b, dims, preferred_element_type=f32)  15.9 us
    all_to_all x1, waiting for transfers between devices, body(): lax.all_to_all(summed.reshape(local_slots, expert_ranks, 2 * width), 'exp...  14.9 us
    ppermute x1, waiting for transfers between devices, body(): lax.ppermute(leaving.astype(bf16), 'context', route).astype(f32)  12.2 us
    ppermute x3, waiting for transfers between devices, body(): lax.ppermute(leaving, 'context', [(r, (r + hop) % ranks) for r in range(r...  11.5 us
    unnamed x95, local copies, waits for them, and re-layouts  11.1 us
    all_gather x1, blocking collectives, share_rows(): return lax.all_gather(rows, 'context', axis=0, tiled=False)  10.1 us
  transfers between devices with their start and end apart: 11, of which 11 were waited for; matrix products, arithmetic and copies ran while one was open for 9% of the time, Pallas kernels for 0%

profile of v3, /device:TPU:0, one launch (start us, length us, event | category | flops | bytes accessed | tf_op | source)
XLA Modules:
  0.0 283.5 jit_solution(7917806675450676217)
XLA Ops:
  8.4 1.7 pad_maximum_fusion.2
  12.7 7.3 %all-to-all-start = ((bf16[20,8,768]{2,0,1:T(8,128)(2,1)}), bf16[20,8,768]{2,0,1:T(8,128)(2,1)S(1)}, u32[]{:S(2)}, u32[]{:S(2)}) async-start(bf16[20,8,768]{2,0,1:T(8,128)(2,1)} %copy.94), calls=%async_computation | async-start | bytes 589824 | tf_op jit(solution)/shard_map/all_to_all | solution.py:224
  20.1 5.8 %copy.96 = bf16[768,2304]{0,1:T(8,128)(2,1)} copy(bf16[768,2304]{1,0:T(8,128)(2,1)} %param.16) | data formatting | bytes 7077888 | tf_op args[3]
  25.9 1.2 constant_dynamic-slice_fusion.4
  27.2 2.5 all-to-all-done
  31.1 1.4 fusion.1
  32.5 1.9 slice.49.ids_ref
  34.4 2.7 convolution_convert_fusion.3
  37.0 2.3 copy.97
  39.3 1.4 slice_bitcast_fusion
  40.7 7.0 %attend.1 = (bf16[3,512,64]{2,1,0:T(8,128)(2,1)S(1)}, bf16[3,512,512]{2,1,0:T(8,128)(2,1)S(1)}) custom-call(bf16[3,512,64]{2,1,0:T(8,128)(2,1)S(1)} %get-tuple-element.37.q_ref, bf16[3,512,64]{2,1,0:T(8,128)(2,1)S(1)} %get-tuple-element.36.k_ref, bf16[3,512,64]{2,1,0:T(8,128)(2,1)S(1)} %get-tuple-element.35.v_ref, ...), custom_call_target="tpu_custom_call" | custom-call | flops 201326592 | bytes 3145728 | tf_op jit(solution)/shard_map/attend/pallas_call | solution.py:123
  49.6 1.8 copy.98
  51.4 8.8 %all_gather.23 = bf16[4,512,192]{1,2,0:T(8,128)(2,1)S(1)} all-gather(bf16[1,512,192]{1,2,0:T(8,128)(2,1)} %bitcast.164), channel_id=1, replica_groups=mesh['experts'=8,'context'=4] {'context'}, dimensions={0}, use_global_device_ids=true | all-gather | bytes 983040 | tf_op jit(solution)/shard_map/all_gather | solution.py:256
  60.2 2.0 multiply_reduce_fusion.2
  63.6 22.4 %all_to_all.25 = bf16[20,8,1536]{2,0,1:T(8,128)(2,1)S(1)} all-to-all(bf16[20,8,1536]{2,0,1:T(8,128)(2,1)S(1)} %copy.99), channel_id=1, replica_groups=mesh['experts'=8,'context'=4] {'experts'}, dimensions={1} | all-to-all | bytes 983040 | tf_op jit(solution)/shard_map/all_to_all | solution.py:224
  86.9 10.1 %all-gather = bf16[640,768]{1,0:T(8,128)(2,1)S(1)} all-gather(bf16[160,768]{1,0:T(8,128)(2,1)} %bitcast.161), channel_id=2, replica_groups=mesh['experts'=8,'context'=4] {'context'}, dimensions={0}, use_global_device_ids=true | all-gather | bytes 1228800 | tf_op jit(solution)/shard_map/all_gather | solution.py:228
  98.0 9.0 %all-gather.6.cloned.1.call-done = bf16[4,160,1536]{2,1,0:T(8,128)(2,1)} async-done(((bf16[1,160,1536]{2,1,0:T(8,128)(2,1)}), bf16[4,160,1536]{2,1,0:T(8,128)(2,1)}) %all-gather.6.cloned.1.call-update) | async-done | bytes 1966096 | tf_op jit(solution)/shard_map/all_gather | solution.py:228
  107.0 1.7 copy.101
  115.1 1.4 copy.103
  116.5 1.3 dynamic-slice_bitcast_fusion
  118.1 2.5 collective-permute-done
  120.5 1.8 convert_add_fusion
  123.2 1.5 collective-permute-start.1
  124.6 12.2 %collective-permute-done.1 = bf16[160,1536]{1,0:T(8,128)(2,1)} collective-permute-done((bf16[160,1536]{1,0:T(8,128)(2,1)}, bf16[160,1536]{1,0:T(8,128)(2,1)}, u32[]{:S(2)}, u32[]{:S(2)}) %collective-permute-start.1) | collective-permute-done | bytes 491552 | tf_op jit(solution)/shard_map/ppermute | solution.py:301
  138.9 5.0 %all-to-all-start.2 = ((bf16[20,8,1536]{2,0,1:T(8,128)(2,1)}), bf16[20,8,1536]{2,0,1:T(8,128)(2,1)S(1)}, u32[]{:S(2)}, u32[]{:S(2)}) async-start(bf16[20,8,1536]{2,0,1:T(8,128)(2,1)} %copy.104), calls=%async_computation.2 | async-start | bytes 1179648 | tf_op jit(solution)/shard_map/all_to_all | solution.py:303
  144.6 14.9 %all-to-all-done.2 = bf16[20,8,1536]{2,0,1:T(8,128)(2,1)S(1)} async-done(((bf16[20,8,1536]{2,0,1:T(8,128)(2,1)}), bf16[20,8,1536]{2,0,1:T(8,128)(2,1)S(1)}, u32[]{:S(2)}, u32[]{:S(2)}) %all-to-all-start.2) | async-done | bytes 491552 | tf_op jit(solution)/shard_map/all_to_all | solution.py:303
  160.2 7.8 %all_gather.27 = bf16[512,768]{1,0:T(8,128)(2,1)S(1)} all-gather(bf16[128,768]{1,0:T(8,128)(2,1)S(1)} %fusion.59), channel_id=1, replica_groups=mesh['experts'=8,'context'=4] {'context'}, dimensions={0}, use_global_device_ids=true | all-gather | bytes 983040 | tf_op jit(solution)/shard_map/all_gather | solution.py:318
  168.0 1.6 convolution_convert_fusion.6
  170.8 6.7 %attend_back.1 = (bf16[3,512,64]{2,1,0:T(8,128)(2,1)S(1)}, bf16[3,512,64]{2,1,0:T(8,128)(2,1)S(1)}, bf16[3,512,64]{2,1,0:T(8,128)(2,1)S(1)}, bf16[3,512,512]{2,1,0:T(8,128)(2,1)S(1)}) custom-call(bf16[3,512,64]{2,1,0:T(8,128)(2,1)S(1)} %get-tuple-element.37.q_ref, bf16[3,512,64]{2,1,0:T(8,128)(2,1)S(1)} %get-tuple-element.36.k_ref, ...), custom_call_target="tpu_custom_call" | custom-call | flops 402653184 | bytes 6291456 | tf_op jit(solution)/shard_map/attend_back/pallas_call | solution.py:147
  178.8 2.8 fusion.39
  181.6 2.4 copy.114
  184.0 2.4 convolution_convert_fusion.4
  186.4 7.8 %table_sums.1 = f32[3,32,512]{2,1,0:T(8,128)S(1)} custom-call(bf16[3,512,512]{2,1,0:T(8,128)(2,1)S(1)} %copy-done.8, bf16[512,512]{1,0:T(8,128)(2,1)S(1)} %copy-done.3), custom_call_target="tpu_custom_call" | custom-call | flops 9437184000 | bytes 3145728 | tf_op jit(solution)/shard_map/table_sums/pallas_call | solution.py:166
  197.0 1.4 collective-permute-start.3
  199.7 5.3 %collective-permute-done.2 = bf16[1,128,576]{1,0,2:T(2,128)(2,1)S(1)} collective-permute-done((bf16[1,128,576]{1,0,2:T(2,128)(2,1)S(1)}, bf16[1,128,576]{1,0,2:T(2,128)(2,1)S(1)}, u32[]{:S(2)}, u32[]{:S(2)}) %collective-permute-start.2) | collective-permute-done | bytes 147488 | tf_op jit(solution)/shard_map/ppermute | solution.py:354
  205.1 1.8 collective-permute-done.3
  206.9 4.4 %collective-permute-done.4 = bf16[1,128,576]{1,0,2:T(2,128)(2,1)S(1)} collective-permute-done((bf16[1,128,576]{1,0,2:T(2,128)(2,1)S(1)}, bf16[1,128,576]{1,0,2:T(2,128)(2,1)S(1)}, u32[]{:S(2)}, u32[]{:S(2)}) %collective-permute-start.4) | collective-permute-done | bytes 147488 | tf_op jit(solution)/shard_map/ppermute | solution.py:354
  211.4 2.6 fusion.24
  214.6 3.6 %all-to-all-start.4 = ((bf16[8,1,96]{2,1,0:T(2,128)(2,1)}), bf16[8,1,96]{2,1,0:T(2,128)(2,1)S(1)}, u32[]{:S(2)}, u32[]{:S(2)}) async-start(bf16[8,1,96]{2,1,0:T(2,128)(2,1)} %convert_element_type.151), calls=%async_computation.4 | async-start | bytes 8192 | tf_op jit(solution)/shard_map/all_to_all | solution.py:363
  218.3 2.7 pad_maximum_fusion.1
  221.0 3.6 %all-to-all-done.4 = bf16[8,1,96]{2,1,0:T(2,128)(2,1)S(1)} async-done(((bf16[8,1,96]{2,1,0:T(2,128)(2,1)}), bf16[8,1,96]{2,1,0:T(2,128)(2,1)S(1)}, u32[]{:S(2)}, u32[]{:S(2)}) %all-to-all-start.4) | async-done | bytes 1568 | tf_op jit(solution)/shard_map/all_to_all | solution.py:363
  224.7 3.6 %all-to-all-start.3 = ((bf16[8,97,768]{2,1,0:T(8,128)(2,1)}), bf16[8,97,768]{2,1,0:T(8,128)(2,1)S(1)}, u32[]{:S(2)}, u32[]{:S(2)}) async-start(bf16[8,97,768]{2,1,0:T(8,128)(2,1)} %pad_maximum_fusion.1), calls=%async_computation.3 | async-start | bytes 2555904 | tf_op jit(solution)/shard_map/all_to_all | solution.py:347
  228.3 5.0 %fusion.7 = f32[2,768,768]{2,1,0:T(8,128)} fusion(bf16[2,320,768]{2,1,0:T(8,128)(2,1)} %copy-done.30, bf16[2,320,1536]{2,1,0:T(8,128)(2,1)S(1)} %bitcast.143), kind=kOutput, calls=%fused_computation.30 | convolution fusion | flops 754974720 | bytes 6684672 | tf_op jit(solution)/shard_map/xnd,xnf->xdf/dot_general | solution.py:311
  233.4 3.6 %fusion.30 = f32[2,768,768]{2,1,0:T(8,128)} fusion(bf16[2,320,768]{2,1,0:T(8,128)(2,1)S(1)} %bitcast.152, bf16[2,320,768]{2,1,0:T(8,128)(2,1)S(1)} %copy-done.29), kind=kOutput, calls=%fused_computation.71 | convolution fusion | flops 756449280 | bytes 6684672 | tf_op jit(solution)/shard_map/xnf,xnd->xfd/dot_general | solution.py:312
  238.2 21.1 %all-to-all-done.3 = bf16[8,97,768]{2,1,0:T(8,128)(2,1)S(1)} async-done(((bf16[8,97,768]{2,1,0:T(8,128)(2,1)}), bf16[8,97,768]{2,1,0:T(8,128)(2,1)S(1)}, u32[]{:S(2)}, u32[]{:S(2)}) %all-to-all-start.3) | async-done | bytes 1191968 | tf_op jit(solution)/shard_map/all_to_all | solution.py:347
  259.5 7.4 %all_gather.28 = bf16[4,98,768]{2,1,0:T(8,128)(2,1)S(1)} all-gather(bf16[1,98,768]{2,1,0:T(8,128)(2,1)S(1)} %pad_maximum_fusion.3), channel_id=1, replica_groups=mesh['experts'=8,'context'=4] {'context'}, dimensions={0}, use_global_device_ids=true | all-gather | bytes 752640 | tf_op jit(solution)/shard_map/all_gather | solution.py:373
  270.5 1.5 copy.120
  272.0 3.0 %reshape_reshape.11 = f32[96,2304]{1,0:T(8,128)} reshape(f32[96,3,4,192]{3,2,1,0:T(4,128)} %copy.120) | data formatting | bytes 1769472 | tf_op jit(solution)/shard_map/reshape;reshape | solution.py:376
  (167 shorter events, 35.2 us)
Async XLA Ops:
  7.2 101.6 %copy-start = (bf16[2,768,768]{2,1,0:T(8,128)(2,1)S(1)}, bf16[2,768,768]{2,1,0:T(8,128)(2,1)}, u32[]{:S(2)}) copy-start(bf16[2,768,768]{2,1,0:T(8,128)(2,1)} %param.23) | copy-start | bytes 7077892
  7.2 23.9 %all-gather.4.cloned.1.call-start = ((), (), s32[]{:S(2)}) async-start(), calls=%async_computation.5 | async-start | bytes 1638400 | tf_op jit(solution)/shard_map/all_gather | solution.py:230
  12.7 16.9 %all-to-all-start = ((bf16[20,8,768]{2,0,1:T(8,128)(2,1)}), bf16[20,8,768]{2,0,1:T(8,128)(2,1)S(1)}, u32[]{:S(2)}, u32[]{:S(2)}) async-start(bf16[20,8,768]{2,0,1:T(8,128)(2,1)} %copy.94), calls=%async_computation | async-start | bytes 589824 | tf_op jit(solution)/shard_map/all_to_all | solution.py:224
  20.0 87.0 %all-gather.6.cloned.1.call-start = ((), (), s32[]{:S(2)}) async-start(), calls=%async_computation.6 | async-start | bytes 2457600 | tf_op jit(solution)/shard_map/all_gather | solution.py:228
  20.1 5.8 %copy-start.33 = (f32[32,12]{0,1:T(8,128)S(1)}, f32[32,12]{0,1:T(8,128)}, u32[]{:S(2)}) copy-start(f32[32,12]{0,1:T(8,128)} %param.18) | copy-start | bytes 4612
  25.9 8.4 %copy-start.32 = (f32[768]{0:T(1024)S(1)}, f32[768]{0:T(1024)}, u32[]{:S(2)}) copy-start(f32[768]{0:T(1024)} %param.14) | copy-start | bytes 9220
  34.4 5.0 %copy-start.39 = (f32[512]{0:T(512)}, f32[512]{0:T(512)S(1)}, u32[]{:S(2)}) copy-start(f32[512]{0:T(512)S(1)} %add_rsqrt_fusion) | copy-start | bytes 6148
  39.3 1.4 copy-start.2
  49.6 13.4 %copy-start.31 = (f32[768]{0:T(1024)S(1)}, f32[768]{0:T(1024)}, u32[]{:S(2)}) copy-start(f32[768]{0:T(1024)} %param.15) | copy-start | bytes 9220
  60.2 2.9 %copy-start.21 = (bf16[4,512,192]{1,2,0:T(8,128)(2,1)}, bf16[4,512,192]{1,2,0:T(8,128)(2,1)S(1)}, u32[]{:S(2)}) copy-start(bf16[4,512,192]{1,2,0:T(8,128)(2,1)S(1)} %all_gather.23) | copy-start | bytes 2359300
  110.0 2.0 copy-start.46
  111.0 2.9 %copy-start.28 = (bf16[2,320,768]{2,1,0:T(8,128)(2,1)}, bf16[2,320,768]{2,1,0:T(8,128)(2,1)S(1)}, u32[]{:S(2)}) copy-start(bf16[2,320,768]{2,1,0:T(8,128)(2,1)S(1)} %get-tuple-element.47) | copy-start | bytes 2949124
  117.8 2.8 collective-permute-start
  123.2 13.7 %collective-permute-start.1 = (bf16[160,1536]{1,0:T(8,128)(2,1)}, bf16[160,1536]{1,0:T(8,128)(2,1)}, u32[]{:S(2)}, u32[]{:S(2)}) collective-permute-start(bf16[160,1536]{1,0:T(8,128)(2,1)} %fusion.11), channel_id=1, source_target_pairs={{0,2},{1,3},{2,0},{3,1},{4,6},{5,7},{6,4},{7,5},{8,10},{9,11},{10,... | collective-permute-start | bytes 1474568 | tf_op jit(solution)/shard_map/ppermute | solution.py:301
  124.6 19.3 %copy-start.17 = (bf16[1,128,768]{2,1,0:T(8,128)(2,1)S(1)}, bf16[1,128,768]{2,1,0:T(8,128)(2,1)}, u32[]{:S(2)}) copy-start(bf16[1,128,768]{2,1,0:T(8,128)(2,1)} %param.13) | copy-start | bytes 589828
  137.9 21.9 %copy-start.11 = (f32[128,768]{1,0:T(8,128)S(1)}, f32[128,768]{1,0:T(8,128)}, u32[]{:S(2)}) copy-start(f32[128,768]{1,0:T(8,128)} %copy-done.10) | copy-start | bytes 1179652
  138.9 21.0 %copy-start.42 = (f32[128]{0:T(128)S(1)}, f32[128]{0:T(128)}, u32[]{:S(2)}) copy-start(f32[128]{0:T(128)} %copy-done.41) | copy-start | bytes 1540
  138.9 21.1 %copy-start.24 = (bf16[1,128,768]{2,1,0:T(8,128)(2,1)S(1)}, bf16[1,128,768]{2,1,0:T(8,128)(2,1)}, u32[]{:S(2)}) copy-start(bf16[1,128,768]{2,1,0:T(8,128)(2,1)} %param.25) | copy-start | bytes 589828
  138.9 20.5 %all-to-all-start.2 = ((bf16[20,8,1536]{2,0,1:T(8,128)(2,1)}), bf16[20,8,1536]{2,0,1:T(8,128)(2,1)S(1)}, u32[]{:S(2)}, u32[]{:S(2)}) async-start(bf16[20,8,1536]{2,0,1:T(8,128)(2,1)} %copy.104), calls=%async_computation.2 | async-start | bytes 1179648 | tf_op jit(solution)/shard_map/all_to_all | solution.py:303
  144.1 15.9 %copy-start.43 = (f32[128]{0:T(128)}, f32[128]{0:T(128)S(1)}, u32[]{:S(2)}) copy-start(f32[128]{0:T(128)S(1)} %fusion.21) | copy-start | bytes 1540
  159.8 9.8 %copy-start.15 = (f32[128,1536]{1,0:T(8,128)}, f32[128,1536]{1,0:T(8,128)S(1)}, u32[]{:S(2)}) copy-start(f32[128,1536]{1,0:T(8,128)S(1)} %fusion.14) | copy-start | bytes 2359300
  160.0 9.8 %copy-start.37 = (f32[128]{0:T(128)}, f32[128]{0:T(128)S(1)}, u32[]{:S(2)}) copy-start(f32[128]{0:T(128)S(1)} %multiply_multiply_fusion.1) | copy-start | bytes 1540
  168.0 1.6 copy-start.20
  181.6 4.8 %copy-start.3 = (bf16[512,512]{1,0:T(8,128)(2,1)S(1)}, bf16[512,512]{1,0:T(8,128)(2,1)}, u32[]{:S(2)}) copy-start(bf16[512,512]{1,0:T(8,128)(2,1)} %slice.49.ids_ref) | copy-start | bytes 1572868
  181.6 4.8 %copy-start.8 = (bf16[3,512,512]{2,1,0:T(8,128)(2,1)S(1)}, bf16[3,512,512]{2,1,0:T(8,128)(2,1)}, u32[]{:S(2)}) copy-start(bf16[3,512,512]{2,1,0:T(8,128)(2,1)} %copy-done.7) | copy-start | bytes 4718596
  195.3 16.0 %copy-start.18 = (bf16[1,128,768]{2,1,0:T(8,128)(2,1)S(1)}, bf16[1,128,768]{2,1,0:T(8,128)(2,1)}, u32[]{:S(2)}) copy-start(bf16[1,128,768]{2,1,0:T(8,128)(2,1)} %param.13) | copy-start | bytes 589828
  196.6 14.8 %copy-start.9 = (bf16[768,2304]{1,0:T(8,128)(2,1)S(1)}, bf16[768,2304]{1,0:T(8,128)(2,1)}, u32[]{:S(2)}) copy-start(bf16[768,2304]{1,0:T(8,128)(2,1)} %param.16) | copy-start | bytes 10616836
  196.6 14.8 %copy-start.35 = (f32[128]{0:T(128)S(1)}, f32[128]{0:T(128)}, u32[]{:S(2)}) copy-start(f32[128]{0:T(128)} %fusion.55) | copy-start | bytes 1540
  196.6 8.4 %collective-permute-start.2 = (bf16[1,128,576]{1,0,2:T(2,128)(2,1)S(1)}, bf16[1,128,576]{1,0,2:T(2,128)(2,1)S(1)}, u32[]{:S(2)}, u32[]{:S(2)}) collective-permute-start(bf16[1,128,576]{1,0,2:T(2,128)(2,1)S(1)} %get-tuple-element.40), channel_id=1, source_target_pairs={{0,1},{1,2},{2,3},{3,0},{4,5},{5,6},{6,7},{7,4},{8,9},{9,10},{10,1... | collective-permute-start | bytes 442376 | tf_op jit(solution)/shard_map/ppermute | solution.py:354
  197.0 9.9 %collective-permute-start.3 = (bf16[1,128,576]{1,0,2:T(2,128)(2,1)S(1)}, bf16[1,128,576]{1,0,2:T(2,128)(2,1)S(1)}, u32[]{:S(2)}, u32[]{:S(2)}) collective-permute-start(bf16[1,128,576]{1,0,2:T(2,128)(2,1)S(1)} %get-tuple-element.39), channel_id=1, source_target_pairs={{0,2},{1,3},{2,0},{3,1},{4,6},{5,7},{6,4},{7,5},{8,10},{9,11},{10,... | collective-permute-start | bytes 442376 | tf_op jit(solution)/shard_map/ppermute | solution.py:354
  198.4 12.8 %collective-permute-start.4 = (bf16[1,128,576]{1,0,2:T(2,128)(2,1)S(1)}, bf16[1,128,576]{1,0,2:T(2,128)(2,1)S(1)}, u32[]{:S(2)}, u32[]{:S(2)}) collective-permute-start(bf16[1,128,576]{1,0,2:T(2,128)(2,1)S(1)} %get-tuple-element.38), channel_id=1, source_target_pairs={{0,3},{1,0},{2,1},{3,2},{4,7},{5,4},{6,5},{7,6},{8,11},{9,8},{10,9... | collective-permute-start | bytes 442376 | tf_op jit(solution)/shard_map/ppermute | solution.py:354
  214.6 10.0 %all-to-all-start.4 = ((bf16[8,1,96]{2,1,0:T(2,128)(2,1)}), bf16[8,1,96]{2,1,0:T(2,128)(2,1)S(1)}, u32[]{:S(2)}, u32[]{:S(2)}) async-start(bf16[8,1,96]{2,1,0:T(2,128)(2,1)} %convert_element_type.151), calls=%async_computation.4 | async-start | bytes 8192 | tf_op jit(solution)/shard_map/all_to_all | solution.py:363
  218.3 10.0 %copy-start.14 = (bf16[2,4,80,1536]{3,2,1,0:T(8,128)(2,1)S(1)}, bf16[2,4,80,1536]{3,2,1,0:T(8,128)(2,1)}, u32[]{:S(2)}) copy-start(bf16[2,4,80,1536]{3,2,1,0:T(8,128)(2,1)} %copy-done.13) | copy-start | bytes 5898244
  224.7 34.6 %all-to-all-start.3 = ((bf16[8,97,768]{2,1,0:T(8,128)(2,1)}), bf16[8,97,768]{2,1,0:T(8,128)(2,1)S(1)}, u32[]{:S(2)}, u32[]{:S(2)}) async-start(bf16[8,97,768]{2,1,0:T(8,128)(2,1)} %pad_maximum_fusion.1), calls=%async_computation.3 | async-start | bytes 2555904 | tf_op jit(solution)/shard_map/all_to_all | solution.py:347
  228.3 5.0 %copy-start.23 = (bf16[2,4,80,768]{3,2,1,0:T(8,128)(2,1)S(1)}, bf16[2,4,80,768]{3,2,1,0:T(8,128)(2,1)}, u32[]{:S(2)}) copy-start(bf16[2,4,80,768]{3,2,1,0:T(8,128)(2,1)} %copy.102) | copy-start | bytes 2949124
  228.3 5.0 %copy-start.29 = (bf16[2,320,768]{2,1,0:T(8,128)(2,1)S(1)}, bf16[2,320,768]{2,1,0:T(8,128)(2,1)}, u32[]{:S(2)}) copy-start(bf16[2,320,768]{2,1,0:T(8,128)(2,1)} %copy-done.28) | copy-start | bytes 2949124
  233.3 3.7 %copy-start.44 = (f32[128]{0:T(128)S(1)}, f32[128]{0:T(128)}, u32[]{:S(2)}) copy-start(f32[128]{0:T(128)} %copy-done.43) | copy-start | bytes 1540
  233.3 3.7 %copy-start.45 = (f32[128]{0:T(128)S(1)}, f32[128]{0:T(128)}, u32[]{:S(2)}) copy-start(f32[128]{0:T(128)} %get-tuple-element.32) | copy-start | bytes 1540
  233.3 3.8 %copy-start.12 = (f32[128,768]{1,0:T(8,128)S(1)}, f32[128,768]{1,0:T(8,128)}, u32[]{:S(2)}) copy-start(f32[128,768]{1,0:T(8,128)} %copy-done.10) | copy-start | bytes 1179652
  233.3 3.8 %copy-start.16 = (f32[128,1536]{1,0:T(8,128)S(1)}, f32[128,1536]{1,0:T(8,128)}, u32[]{:S(2)}) copy-start(f32[128,1536]{1,0:T(8,128)} %copy-done.15) | copy-start | bytes 2359300
  233.3 3.8 %copy-start.19 = (bf16[1,128,768]{2,1,0:T(8,128)(2,1)S(1)}, bf16[1,128,768]{2,1,0:T(8,128)(2,1)}, u32[]{:S(2)}) copy-start(bf16[1,128,768]{2,1,0:T(8,128)(2,1)} %param.13) | copy-start | bytes 589828
  233.3 3.7 %copy-start.25 = (bf16[1,128,768]{2,1,0:T(8,128)(2,1)S(1)}, bf16[1,128,768]{2,1,0:T(8,128)(2,1)}, u32[]{:S(2)}) copy-start(bf16[1,128,768]{2,1,0:T(8,128)(2,1)} %param.25) | copy-start | bytes 589828
  233.3 3.7 %copy-start.27 = (f32[128,768]{1,0:T(8,128)S(1)}, f32[128,768]{1,0:T(8,128)}, u32[]{:S(2)}) copy-start(f32[128,768]{1,0:T(8,128)} %get-tuple-element.48) | copy-start | bytes 1179652
  233.3 3.7 %copy-start.34 = (f32[1,128]{1,0:T(1,128)S(1)}, f32[1,128]{1,0:T(1,128)}, u32[]{:S(2)}) copy-start(f32[1,128]{1,0:T(1,128)} %param.22) | copy-start | bytes 1540
  233.3 3.7 %copy-start.36 = (f32[128]{0:T(128)S(1)}, f32[128]{0:T(128)}, u32[]{:S(2)}) copy-start(f32[128]{0:T(128)} %fusion.55) | copy-start | bytes 1540
  233.3 3.7 %copy-start.38 = (f32[128]{0:T(128)S(1)}, f32[128]{0:T(128)}, u32[]{:S(2)}) copy-start(f32[128]{0:T(128)} %copy-done.37) | copy-start | bytes 1540
  270.5 6.2 %copy-start.1 = (bf16[2,768,768]{2,1,0:T(8,128)(2,1)S(1)}, bf16[2,768,768]{2,1,0:T(8,128)(2,1)}, u32[]{:S(2)}) copy-start(bf16[2,768,768]{2,1,0:T(8,128)(2,1)} %param.23) | copy-start | bytes 7077892
  272.0 3.7 %copy-start.26 = (f32[4,96,192]{1,2,0:T(8,128)S(1)}, f32[4,96,192]{1,2,0:T(8,128)}, u32[]{:S(2)}) copy-start(f32[4,96,192]{1,2,0:T(8,128)} %slice.68) | copy-start | bytes 884740
  (10 other events, 9.8 us)
Sparse Core Ops, SparseCore 0:
  10.2 20.8 all-gather.3
  87.0 19.9 all-gather.5

commit v4 on v3

--- a/solution.py
+++ b/solution.py
@@ -327,6 +327,7 @@
     my_d_middle = lax.dynamic_slice_in_dim(all_d_middle, me * columns, columns, 1)
     qkv_part = dot(normed, d_qkv, TN)
     proj_part = dot(all_att, my_d_middle, TN)
+    first_piece = jnp.sum(my_weight.astype(f32) * qkv_part, axis=1) / first_gain
     d_scores, qkv_part = lax.optimization_barrier((d_scores, qkv_part))
     table_part = table_sums(d_scores, ids, buckets).T
     wide_part = jnp.concatenate([qkv_part, proj_part], axis=1).astype(bf16)
@@ -335,6 +336,7 @@
     table_out = buckets // expert_ranks
     small = jnp.concatenate(
         [
+            first_piece.reshape(expert_ranks, rows_out),
             second_part.reshape(expert_ranks, rows_out),
             table_part.reshape(expert_ranks, table_out * group),
         ],
@@ -345,6 +347,7 @@
         [wide_part.reshape(expert_ranks, rows_out, grad_width), small[:, None, :]], axis=1
     )
     sums = lax.all_to_all(wide_part, "experts", split_axis=0, concat_axis=0, tiled=True)
+    d_qkv, _ = lax.optimization_barrier((d_qkv, wide_part))
     outgoing = d_qkv.reshape(ranks, local_rows, 3 * share)
     own = lax.dynamic_update_index_in_dim(
         jnp.zeros_like(outgoing), lax.dynamic_index_in_dim(outgoing, me, 0), me, 0
@@ -356,29 +359,20 @@
     own = own.reshape(ranks, local_rows, 3, share).transpose(1, 2, 0, 3)
     own = own.reshape(local_rows, 3, ranks * share)[:, :, :width].reshape(local_rows, 3 * width)
     d_first = dot(own, qkv_weight, NT)
-    _, first_pull = jax.vjp(rms_scale, features, first_gain)
-    d_input_norm, first_part = first_pull(d_first)
+    _, first_pull = jax.vjp(lambda values: rms_scale(values, first_gain), features)
+    (d_input_norm,) = first_pull(d_first)
     input_grad = (d_middle + d_input_norm)[None]
 
-    first_rows = lax.all_to_all(
-        first_part.astype(bf16).reshape(expert_ranks, 1, rows_out),
-        "experts",
-        split_axis=0,
-        concat_axis=0,
-        tiled=True,
-    )
-    first_sum = jnp.sum(first_rows.astype(f32), axis=0)
-    first_row = jnp.pad(first_sum, ((0, 0), (0, grad_width - rows_out)))
-    sums = jnp.concatenate([jnp.sum(sums.astype(f32), axis=0), first_row], axis=0).astype(bf16)
+    sums = jnp.sum(sums.astype(f32), axis=0).astype(bf16)
     full = lax.all_gather(sums, "context", axis=0, tiled=False).astype(f32)
     qkv_grad = full[:, :rows_out, : 3 * share].reshape(ranks, rows_out, 3, share)
     qkv_grad = qkv_grad.transpose(1, 2, 0, 3).reshape(rows_out, 3, ranks * share)
     qkv_grad = qkv_grad[:, :, :width].reshape(rows_out, 3 * width)
     proj_grad = full[:, :rows_out, 3 * share :].transpose(1, 0, 2).reshape(rows_out, width)
     last = full[:, rows_out]
-    first_grad = jnp.sum(full[:, rows_out + 1, :rows_out], axis=0)
-    second_grad = jnp.sum(last[:, :rows_out], axis=0)
-    table_grad = last[:, rows_out : rows_out + table_out * group]
+    first_grad = jnp.sum(last[:, :rows_out], axis=0)
+    second_grad = jnp.sum(last[:, rows_out : 2 * rows_out], axis=0)
+    table_grad = last[:, 2 * rows_out : 2 * rows_out + table_out * group]
     table_grad = table_grad.reshape(ranks, table_out, group).transpose(1, 0, 2)
     table_grad = table_grad.reshape(table_out, ranks * group)[:, :heads]
     return (

time: 285 us -> 261 us (0.916)
  waiting for transfers between devices: 78 us -> 57.8 us
    all_to_all x1, waiting for transfers between devices: 21.1 us -> 10.4 us  [body(): lax.all_to_all(wide_part, 'experts', split_axis=0, concat_axis=0, tiled=T...]
    ppermute x3, waiting for transfers between devices: 11.5 us -> 5.01 us  [body(): lax.ppermute(leaving, 'context', [(r, (r + hop) % ranks) for r in range(r...]
    all_to_all x1 -> x0, waiting for transfers between devices: 3.64 us -> none  [body(): lax.all_to_all(first_part.astype(bf16).reshape(expert_ranks, 1, rows_out)...]
    all_to_all x1 -> x0, starting transfers between devices: 3.64 us -> none  [body(): lax.all_to_all(first_part.astype(bf16).reshape(expert_ranks, 1, rows_out)...]
    unnamed x95 -> x90, local copies, waits for them, and re-layouts: 11.1 us -> 11 us
  transfers between devices with their start and end apart: 11 -> 10, of which waited for: 11 -> 10; matrix products, arithmetic and copies ran while one was open for 9% -> 9% of each run, Pallas kernels for 0% -> 0%
where the time goes in v4:
time: 261 us; the launch traced here: 259 us
  waiting for transfers between devices  57.8 us (22%)
  blocking collectives  57 us (22%)
  local copies, waits for them, and re-layouts  43.7 us (17%)
  matrix products  28.5 us (11%)
  starting transfers between devices  21.6 us (8%)
  Pallas kernels  21.4 us (8%)
  between operations  14.7 us (6%)
  other arithmetic  14.6 us (6%)
    all_to_all x1, blocking collectives, send_rows(): lax.all_to_all(spread, 'experts', split_axis=1, concat_axis=1, tiled=True)  22.4 us
    all_to_all x1, waiting for transfers between devices, body(): lax.all_to_all(summed.reshape(local_slots, expert_ranks, 2 * width), 'exp...  15.5 us
    dot_general x9, matrix products, dot(): return lax.dot_general(a, b, dims, preferred_element_type=f32)  15 us
    ppermute x1, waiting for transfers between devices, body(): lax.ppermute(leaving.astype(bf16), 'context', route).astype(f32)  12.2 us
    unnamed x90, local copies, waits for them, and re-layouts  11 us
    all_to_all x1, waiting for transfers between devices, body(): lax.all_to_all(wide_part, 'experts', split_axis=0, concat_axis=0, tiled=T...  10.4 us
    all_gather x1, blocking collectives, share_rows(): return lax.all_gather(rows, 'context', axis=0, tiled=False)  10 us
    all_gather x1, waiting for transfers between devices, share_rows(): return lax.all_gather(rows, 'context', axis=0, tiled=False)  9.02 us
  transfers between devices with their start and end apart: 10, of which 10 were waited for; matrix products, arithmetic and copies ran while one was open for 9% of the time, Pallas kernels for 0%

profile of v4, /device:TPU:0, one launch (start us, length us, event | category | flops | bytes accessed | tf_op | source)
XLA Modules:
  0.0 259.3 jit_solution(3336421758351396975)
XLA Ops:
  8.4 1.7 pad_maximum_fusion.2
  12.7 7.3 %all-to-all-start = ((bf16[20,8,768]{2,0,1:T(8,128)(2,1)}), bf16[20,8,768]{2,0,1:T(8,128)(2,1)S(1)}, u32[]{:S(2)}, u32[]{:S(2)}) async-start(bf16[20,8,768]{2,0,1:T(8,128)(2,1)} %copy.91), calls=%async_computation | async-start | bytes 589824 | tf_op jit(solution)/shard_map/all_to_all | solution.py:224
  20.1 5.8 %copy.93 = bf16[768,2304]{0,1:T(8,128)(2,1)} copy(bf16[768,2304]{1,0:T(8,128)(2,1)} %param.16) | data formatting | bytes 7077888 | tf_op args[3]
  25.9 1.2 constant_dynamic-slice_fusion.4
  27.2 2.4 all-to-all-done
  31.1 1.4 fusion.1
  32.5 1.9 slice.49.ids_ref
  34.4 2.7 %convolution_convert_fusion.3 = bf16[512,576]{0,1:T(8,128)(2,1)} fusion(bf16[768,576]{0,1:T(8,128)(2,1)S(1)} %bitcast.158, f32[768]{0:T(1024)S(1)} %copy-done.33, f32[512]{0:T(512)S(1)} %add_rsqrt_fusion, bf16[512,1280]{1,0:T(8,128)(2,1)} %all-gather.6.cloned.1.call-done), kind=kOutput, calls=%fused_computation.18 | convolution fusion | flops 454852608 | bytes 2266112 | tf_op jit(solution)/shard_map/dot_general | solution.py:25
  37.1 2.3 copy.94
  39.3 1.4 slice_bitcast_fusion
  40.7 7.0 %attend.1 = (bf16[3,512,64]{2,1,0:T(8,128)(2,1)S(1)}, bf16[3,512,512]{2,1,0:T(8,128)(2,1)S(1)}) custom-call(bf16[3,512,64]{2,1,0:T(8,128)(2,1)S(1)} %get-tuple-element.41.q_ref, bf16[3,512,64]{2,1,0:T(8,128)(2,1)S(1)} %get-tuple-element.40.k_ref, bf16[3,512,64]{2,1,0:T(8,128)(2,1)S(1)} %get-tuple-element.39.v_ref, ...), custom_call_target="tpu_custom_call" | custom-call | flops 201326592 | bytes 3145728 | tf_op jit(solution)/shard_map/attend/pallas_call | solution.py:123
  47.7 1.2 copy-done.4
  49.7 1.8 copy.95
  51.5 8.8 %all_gather.25 = bf16[4,512,192]{1,2,0:T(8,128)(2,1)S(1)} all-gather(bf16[1,512,192]{1,2,0:T(8,128)(2,1)} %bitcast.160), channel_id=1, replica_groups=mesh['experts'=8,'context'=4] {'context'}, dimensions={0}, use_global_device_ids=true | all-gather | bytes 983040 | tf_op jit(solution)/shard_map/all_gather | solution.py:256
  60.3 2.0 multiply_reduce_fusion.3
  63.7 22.4 %all_to_all.20 = bf16[20,8,1536]{2,0,1:T(8,128)(2,1)S(1)} all-to-all(bf16[20,8,1536]{2,0,1:T(8,128)(2,1)S(1)} %copy.96), channel_id=1, replica_groups=mesh['experts'=8,'context'=4] {'experts'}, dimensions={1} | all-to-all | bytes 983040 | tf_op jit(solution)/shard_map/all_to_all | solution.py:224
  87.0 10.0 %all-gather = bf16[640,768]{1,0:T(8,128)(2,1)S(1)} all-gather(bf16[160,768]{1,0:T(8,128)(2,1)} %bitcast.157), channel_id=2, replica_groups=mesh['experts'=8,'context'=4] {'context'}, dimensions={0}, use_global_device_ids=true | all-gather | bytes 1228800 | tf_op jit(solution)/shard_map/all_gather | solution.py:228
  98.1 9.0 %all-gather.8.cloned.1.call-done = bf16[4,160,1536]{2,1,0:T(8,128)(2,1)} async-done(((bf16[1,160,1536]{2,1,0:T(8,128)(2,1)}), bf16[4,160,1536]{2,1,0:T(8,128)(2,1)}) %all-gather.8.cloned.1.call-update) | async-done | bytes 1966096 | tf_op jit(solution)/shard_map/all_gather | solution.py:228
  107.1 1.7 copy.98
  115.2 1.4 copy.100
  116.6 1.3 dynamic-slice_bitcast_fusion
  118.2 2.5 collective-permute-done
  120.6 1.8 convert_add_fusion
  123.2 1.5 collective-permute-start.1
  124.7 12.2 %collective-permute-done.1 = bf16[160,1536]{1,0:T(8,128)(2,1)} collective-permute-done((bf16[160,1536]{1,0:T(8,128)(2,1)}, bf16[160,1536]{1,0:T(8,128)(2,1)}, u32[]{:S(2)}, u32[]{:S(2)}) %collective-permute-start.1) | collective-permute-done | bytes 491552 | tf_op jit(solution)/shard_map/ppermute | solution.py:301
  139.0 5.0 %all-to-all-start.2 = ((bf16[20,8,1536]{2,0,1:T(8,128)(2,1)}), bf16[20,8,1536]{2,0,1:T(8,128)(2,1)S(1)}, u32[]{:S(2)}, u32[]{:S(2)}) async-start(bf16[20,8,1536]{2,0,1:T(8,128)(2,1)} %copy.101), calls=%async_computation.2 | async-start | bytes 1179648 | tf_op jit(solution)/shard_map/all_to_all | solution.py:303
  144.1 15.5 %all-to-all-done.2 = bf16[20,8,1536]{2,0,1:T(8,128)(2,1)S(1)} async-done(((bf16[20,8,1536]{2,0,1:T(8,128)(2,1)}), bf16[20,8,1536]{2,0,1:T(8,128)(2,1)S(1)}, u32[]{:S(2)}, u32[]{:S(2)}) %all-to-all-start.2) | async-done | bytes 491552 | tf_op jit(solution)/shard_map/all_to_all | solution.py:303
  160.3 7.8 %all_gather.29 = bf16[512,768]{1,0:T(8,128)(2,1)S(1)} all-gather(bf16[128,768]{1,0:T(8,128)(2,1)S(1)} %fusion.59), channel_id=1, replica_groups=mesh['experts'=8,'context'=4] {'context'}, dimensions={0}, use_global_device_ids=true | all-gather | bytes 983040 | tf_op jit(solution)/shard_map/all_gather | solution.py:318
  168.1 1.6 convolution_convert_fusion.6
  170.9 6.7 %attend_back.1 = (bf16[3,512,64]{2,1,0:T(8,128)(2,1)S(1)}, bf16[3,512,64]{2,1,0:T(8,128)(2,1)S(1)}, bf16[3,512,64]{2,1,0:T(8,128)(2,1)S(1)}, bf16[3,512,512]{2,1,0:T(8,128)(2,1)S(1)}) custom-call(bf16[3,512,64]{2,1,0:T(8,128)(2,1)S(1)} %get-tuple-element.41.q_ref, bf16[3,512,64]{2,1,0:T(8,128)(2,1)S(1)} %get-tuple-element.40.k_ref, ...), custom_call_target="tpu_custom_call" | custom-call | flops 402653184 | bytes 6291456 | tf_op jit(solution)/shard_map/attend_back/pallas_call | solution.py:147
  177.9 1.3 copy.104
  179.2 3.3 %multiply_reduce_fusion = (f32[768]{0:T(1024)S(1)}, bf16[768,576]{0,1:T(8,128)(2,1)}) fusion(bf16[768,3,192]{0,2,1:T(8,128)(2,1)} %copy-done.31, bf16[512,576]{0,1:T(8,128)(2,1)} %bitcast.151, f32[768]{0:T(1024)S(1)} %copy-done.33, f32[512]{0:T(512)S(1)} %copy-done.39, bf16[512,1280]{1,0:T(8,128)(2,1)} %all-gather.6.cloned.1.call-done), kind=kOutput, calls=%fused_computation.10 | convolution fusion | flops 456326400 | bytes 3153920 | tf_op jit(solution)/shard_map/dot_general | solution.py:25
  182.6 2.4 copy.105
  185.0 2.2 convolution_convert_fusion.4
  187.2 7.8 %table_sums.1 = f32[3,32,512]{2,1,0:T(8,128)S(1)} custom-call(bf16[3,512,512]{2,1,0:T(8,128)(2,1)S(1)} %copy-done.8, bf16[512,512]{1,0:T(8,128)(2,1)S(1)} %copy-done.3), custom_call_target="tpu_custom_call" | custom-call | flops 9437184000 | bytes 3145728 | tf_op jit(solution)/shard_map/table_sums/pallas_call | solution.py:166
  195.7 2.5 pad_maximum_fusion.1
  198.2 4.3 %all-to-all-start.3 = ((bf16[8,97,768]{2,1,0:T(8,128)(2,1)}), bf16[8,97,768]{2,1,0:T(8,128)(2,1)}, u32[]{:S(2)}, u32[]{:S(2)}) async-start(bf16[8,97,768]{2,1,0:T(8,128)(2,1)} %pad_maximum_fusion.1), calls=%async_computation.3 | async-start | bytes 2555904 | tf_op jit(solution)/shard_map/all_to_all | solution.py:349
  202.5 5.0 %fusion.7 = f32[2,768,768]{2,1,0:T(8,128)} fusion(bf16[2,320,768]{2,1,0:T(8,128)(2,1)} %copy-done.30, bf16[2,320,1536]{2,1,0:T(8,128)(2,1)S(1)} %bitcast.138), kind=kOutput, calls=%fused_computation.32 | convolution fusion | flops 754974720 | bytes 6684672 | tf_op jit(solution)/shard_map/xnd,xnf->xdf/dot_general | solution.py:311
  207.5 3.6 %fusion.28 = f32[2,768,768]{2,1,0:T(8,128)} fusion(bf16[2,320,768]{2,1,0:T(8,128)(2,1)S(1)} %bitcast.146, bf16[2,320,768]{2,1,0:T(8,128)(2,1)S(1)} %copy-done.29), kind=kOutput, calls=%fused_computation.70 | convolution fusion | flops 756449280 | bytes 6684672 | tf_op jit(solution)/shard_map/xnf,xnd->xfd/dot_general | solution.py:312
  212.9 1.5 collective-permute-start.3
  215.8 1.9 collective-permute-done.2
  217.7 2.0 collective-permute-done.3
  221.0 1.4 fusion.21
  223.6 10.4 %all-to-all-done.3 = bf16[8,97,768]{2,1,0:T(8,128)(2,1)} async-done(((bf16[8,97,768]{2,1,0:T(8,128)(2,1)}), bf16[8,97,768]{2,1,0:T(8,128)(2,1)}, u32[]{:S(2)}, u32[]{:S(2)}) %all-to-all-start.3) | async-done | bytes 1191968 | tf_op jit(solution)/shard_map/all_to_all | solution.py:349
  233.9 1.5 reduce_sum.126
  235.4 8.0 %all-gather.2 = bf16[4,97,768]{2,1,0:T(8,128)(2,1)S(1)} all-gather(bf16[1,97,768]{2,1,0:T(8,128)(2,1)S(1)} %bitcast.161), channel_id=3, replica_groups=mesh['experts'=8,'context'=4] {'context'}, dimensions={0}, use_global_device_ids=true | all-gather | bytes 744960 | tf_op jit(solution)/shard_map/all_gather | solution.py:367
  246.3 1.5 copy.115
  247.9 3.0 %reshape_reshape.7 = f32[96,2304]{1,0:T(8,128)} reshape(f32[96,3,4,192]{3,2,1,0:T(4,128)} %copy.115) | data formatting | bytes 1769472 | tf_op jit(solution)/shard_map/reshape;reshape | solution.py:370
  (155 shorter events, 31.7 us)
Async XLA Ops:
  7.2 101.7 %copy-start = (bf16[2,768,768]{2,1,0:T(8,128)(2,1)S(1)}, bf16[2,768,768]{2,1,0:T(8,128)(2,1)}, u32[]{:S(2)}) copy-start(bf16[2,768,768]{2,1,0:T(8,128)(2,1)} %param.23) | copy-start | bytes 7077892
  7.2 23.9 %all-gather.6.cloned.1.call-start = ((), (), s32[]{:S(2)}) async-start(), calls=%async_computation.4 | async-start | bytes 1638400 | tf_op jit(solution)/shard_map/all_gather | solution.py:230
  12.7 16.9 %all-to-all-start = ((bf16[20,8,768]{2,0,1:T(8,128)(2,1)}), bf16[20,8,768]{2,0,1:T(8,128)(2,1)S(1)}, u32[]{:S(2)}, u32[]{:S(2)}) async-start(bf16[20,8,768]{2,0,1:T(8,128)(2,1)} %copy.91), calls=%async_computation | async-start | bytes 589824 | tf_op jit(solution)/shard_map/all_to_all | solution.py:224
  20.0 87.1 %all-gather.8.cloned.1.call-start = ((), (), s32[]{:S(2)}) async-start(), calls=%async_computation.5 | async-start | bytes 2457600 | tf_op jit(solution)/shard_map/all_gather | solution.py:228
  20.1 5.8 %copy-start.34 = (f32[32,12]{0,1:T(8,128)S(1)}, f32[32,12]{0,1:T(8,128)}, u32[]{:S(2)}) copy-start(f32[32,12]{0,1:T(8,128)} %param.18) | copy-start | bytes 4612
  25.9 8.4 %copy-start.33 = (f32[768]{0:T(1024)S(1)}, f32[768]{0:T(1024)}, u32[]{:S(2)}) copy-start(f32[768]{0:T(1024)} %param.14) | copy-start | bytes 9220
  27.2 9.9 %copy-start.31 = (bf16[768,3,192]{0,2,1:T(8,128)(2,1)}, bf16[768,3,192]{0,2,1:T(8,128)(2,1)S(1)}, u32[]{:S(2)}) copy-start(bf16[768,3,192]{0,2,1:T(8,128)(2,1)S(1)} %constant_dynamic-slice_fusion.4) | copy-start | bytes 2654212
  34.4 5.0 %copy-start.38 = (f32[512]{0:T(512)}, f32[512]{0:T(512)S(1)}, u32[]{:S(2)}) copy-start(f32[512]{0:T(512)S(1)} %add_rsqrt_fusion) | copy-start | bytes 6148
  39.3 1.4 copy-start.2
  47.7 1.2 copy-start.4
  49.7 13.4 %copy-start.32 = (f32[768]{0:T(1024)S(1)}, f32[768]{0:T(1024)}, u32[]{:S(2)}) copy-start(f32[768]{0:T(1024)} %param.15) | copy-start | bytes 9220
  60.3 2.9 %copy-start.18 = (bf16[4,512,192]{1,2,0:T(8,128)(2,1)}, bf16[4,512,192]{1,2,0:T(8,128)(2,1)S(1)}, u32[]{:S(2)}) copy-start(bf16[4,512,192]{1,2,0:T(8,128)(2,1)S(1)} %all_gather.25) | copy-start | bytes 2359300
  108.8 1.3 copy-start.13
  110.1 1.2 copy-start.20
  110.1 2.0 copy-start.42
  111.1 2.9 %copy-start.28 = (bf16[2,320,768]{2,1,0:T(8,128)(2,1)}, bf16[2,320,768]{2,1,0:T(8,128)(2,1)S(1)}, u32[]{:S(2)}) copy-start(bf16[2,320,768]{2,1,0:T(8,128)(2,1)S(1)} %get-tuple-element.53) | copy-start | bytes 2949124
  117.9 2.8 %collective-permute-start = (bf16[2,160,1536]{2,1,0:T(8,128)(2,1)S(1)}, bf16[2,160,1536]{2,1,0:T(8,128)(2,1)}, u32[]{:S(2)}, u32[]{:S(2)}) collective-permute-start(bf16[2,160,1536]{2,1,0:T(8,128)(2,1)S(1)} %dynamic-slice_bitcast_fusion), channel_id=1, source_target_pairs={{0,1},{1,0},{2,3},{3,2},{4,5},{5,4},{6,7},{7,6},{8,9},{9,8},{10,11... | collective-permute-start | bytes 2949128 | tf_op jit(solution)/shard_map/ppermute | solution.py:295
  123.2 13.7 %collective-permute-start.1 = (bf16[160,1536]{1,0:T(8,128)(2,1)}, bf16[160,1536]{1,0:T(8,128)(2,1)}, u32[]{:S(2)}, u32[]{:S(2)}) collective-permute-start(bf16[160,1536]{1,0:T(8,128)(2,1)} %fusion.11), channel_id=1, source_target_pairs={{0,2},{1,3},{2,0},{3,1},{4,6},{5,7},{6,4},{7,5},{8,10},{9,11},{10,... | collective-permute-start | bytes 1474568 | tf_op jit(solution)/shard_map/ppermute | solution.py:301
  138.0 21.9 %copy-start.11 = (f32[128,768]{1,0:T(8,128)S(1)}, f32[128,768]{1,0:T(8,128)}, u32[]{:S(2)}) copy-start(f32[128,768]{1,0:T(8,128)} %copy-done.10) | copy-start | bytes 1179652
  139.0 21.1 %copy-start.41 = (f32[128]{0:T(128)S(1)}, f32[128]{0:T(128)}, u32[]{:S(2)}) copy-start(f32[128]{0:T(128)} %copy-done.40) | copy-start | bytes 1540
  139.0 21.1 %copy-start.25 = (bf16[1,128,768]{2,1,0:T(8,128)(2,1)S(1)}, bf16[1,128,768]{2,1,0:T(8,128)(2,1)}, u32[]{:S(2)}) copy-start(bf16[1,128,768]{2,1,0:T(8,128)(2,1)} %param.25) | copy-start | bytes 589828
  139.0 20.6 %all-to-all-start.2 = ((bf16[20,8,1536]{2,0,1:T(8,128)(2,1)}), bf16[20,8,1536]{2,0,1:T(8,128)(2,1)S(1)}, u32[]{:S(2)}, u32[]{:S(2)}) async-start(bf16[20,8,1536]{2,0,1:T(8,128)(2,1)} %copy.101), calls=%async_computation.2 | async-start | bytes 1179648 | tf_op jit(solution)/shard_map/all_to_all | solution.py:303
  159.9 9.8 %copy-start.15 = (f32[128,1536]{1,0:T(8,128)}, f32[128,1536]{1,0:T(8,128)S(1)}, u32[]{:S(2)}) copy-start(f32[128,1536]{1,0:T(8,128)S(1)} %fusion.14) | copy-start | bytes 2359300
  160.1 9.8 %copy-start.36 = (f32[128]{0:T(128)}, f32[128]{0:T(128)S(1)}, u32[]{:S(2)}) copy-start(f32[128]{0:T(128)S(1)} %multiply_multiply_fusion.1) | copy-start | bytes 1540
  168.1 1.6 copy-start.17
  177.6 1.6 copy-start.7
  177.6 1.6 copy-start.39
  179.2 5.8 %copy-start.19 = (bf16[4,512,192]{1,2,0:T(8,128)(2,1)S(1)}, bf16[4,512,192]{1,2,0:T(8,128)(2,1)}, u32[]{:S(2)}) copy-start(bf16[4,512,192]{1,2,0:T(8,128)(2,1)} %copy-done.18) | copy-start | bytes 2359300
  182.6 4.7 %copy-start.3 = (bf16[512,512]{1,0:T(8,128)(2,1)S(1)}, bf16[512,512]{1,0:T(8,128)(2,1)}, u32[]{:S(2)}) copy-start(bf16[512,512]{1,0:T(8,128)(2,1)} %slice.49.ids_ref) | copy-start | bytes 1572868
  182.6 4.7 %copy-start.8 = (bf16[3,512,512]{2,1,0:T(8,128)(2,1)S(1)}, bf16[3,512,512]{2,1,0:T(8,128)(2,1)}, u32[]{:S(2)}) copy-start(bf16[3,512,512]{2,1,0:T(8,128)(2,1)} %copy-done.7) | copy-start | bytes 4718596
  187.2 8.4 %copy-start.22 = (bf16[768,576]{1,0:T(8,128)(2,1)S(1)}, bf16[768,576]{1,0:T(8,128)(2,1)}, u32[]{:S(2)}) copy-start(bf16[768,576]{1,0:T(8,128)(2,1)} %copy.105) | copy-start | bytes 2654212
  195.6 6.8 %copy-start.14 = (bf16[2,4,80,1536]{3,2,1,0:T(8,128)(2,1)S(1)}, bf16[2,4,80,1536]{3,2,1,0:T(8,128)(2,1)}, u32[]{:S(2)}) copy-start(bf16[2,4,80,1536]{3,2,1,0:T(8,128)(2,1)} %copy-done.13) | copy-start | bytes 5898244
  198.2 35.8 %all-to-all-start.3 = ((bf16[8,97,768]{2,1,0:T(8,128)(2,1)}), bf16[8,97,768]{2,1,0:T(8,128)(2,1)}, u32[]{:S(2)}, u32[]{:S(2)}) async-start(bf16[8,97,768]{2,1,0:T(8,128)(2,1)} %pad_maximum_fusion.1), calls=%async_computation.3 | async-start | bytes 2555904 | tf_op jit(solution)/shard_map/all_to_all | solution.py:349
  202.5 5.0 %copy-start.21 = (bf16[2,4,80,768]{3,2,1,0:T(8,128)(2,1)S(1)}, bf16[2,4,80,768]{3,2,1,0:T(8,128)(2,1)}, u32[]{:S(2)}) copy-start(bf16[2,4,80,768]{3,2,1,0:T(8,128)(2,1)} %copy.99) | copy-start | bytes 2949124
  202.5 5.0 %copy-start.29 = (bf16[2,320,768]{2,1,0:T(8,128)(2,1)S(1)}, bf16[2,320,768]{2,1,0:T(8,128)(2,1)}, u32[]{:S(2)}) copy-start(bf16[2,320,768]{2,1,0:T(8,128)(2,1)} %copy-done.28) | copy-start | bytes 2949124
  207.5 3.6 %copy-start.24 = (bf16[512,3,3,64]{0,3,2,1:T(8,128)(2,1)S(1)}, bf16[512,3,3,64]{0,3,2,1:T(8,128)(2,1)}, u32[]{:S(2)}) copy-start(bf16[512,3,3,64]{0,3,2,1:T(8,128)(2,1)} %copy.104) | copy-start | bytes 1769476
  212.5 5.2 %collective-permute-start.2 = (bf16[1,128,576]{1,2,0:T(8,128)(2,1)S(1)}, bf16[1,128,576]{1,2,0:T(8,128)(2,1)S(1)}, u32[]{:S(2)}, u32[]{:S(2)}) collective-permute-start(bf16[1,128,576]{1,2,0:T(8,128)(2,1)S(1)} %copy.122), channel_id=1, source_target_pairs={{0,1},{1,2},{2,3},{3,0},{4,5},{5,6},{6,7},{7,4},{8,9},{9,10},{10,1... | collective-permute-start | bytes 442376 | tf_op jit(solution)/shard_map/ppermute | solution.py:357
  212.9 8.0 %copy-start.9 = (bf16[768,2304]{1,0:T(8,128)(2,1)S(1)}, bf16[768,2304]{1,0:T(8,128)(2,1)}, u32[]{:S(2)}) copy-start(bf16[768,2304]{1,0:T(8,128)(2,1)} %param.16) | copy-start | bytes 10616836
  212.9 8.0 %copy-start.23 = (bf16[1,128,768]{2,1,0:T(8,128)(2,1)S(1)}, bf16[1,128,768]{2,1,0:T(8,128)(2,1)}, u32[]{:S(2)}) copy-start(bf16[1,128,768]{2,1,0:T(8,128)(2,1)} %param.13) | copy-start | bytes 589828
  212.9 6.8 %collective-permute-start.3 = (bf16[1,128,576]{1,2,0:T(8,128)(2,1)S(1)}, bf16[1,128,576]{1,2,0:T(8,128)(2,1)S(1)}, u32[]{:S(2)}, u32[]{:S(2)}) collective-permute-start(bf16[1,128,576]{1,2,0:T(8,128)(2,1)S(1)} %copy.123), channel_id=1, source_target_pairs={{0,2},{1,3},{2,0},{3,1},{4,6},{5,7},{6,4},{7,5},{8,10},{9,11},{10,... | collective-permute-start | bytes 442376 | tf_op jit(solution)/shard_map/ppermute | solution.py:357
  214.5 6.4 %collective-permute-start.4 = (bf16[1,128,576]{1,2,0:T(8,128)(2,1)S(1)}, bf16[1,128,576]{1,2,0:T(8,128)(2,1)S(1)}, u32[]{:S(2)}, u32[]{:S(2)}) collective-permute-start(bf16[1,128,576]{1,2,0:T(8,128)(2,1)S(1)} %copy.124), channel_id=1, source_target_pairs={{0,3},{1,0},{2,1},{3,2},{4,7},{5,4},{6,5},{7,6},{8,11},{9,8},{10,9... | collective-permute-start | bytes 442376 | tf_op jit(solution)/shard_map/ppermute | solution.py:357
  221.0 1.5 copy-start.12
  221.0 1.5 copy-start.16
  221.0 1.5 copy-start.26
  221.0 1.5 copy-start.35
  221.0 1.5 copy-start.37
  246.3 6.2 %copy-start.1 = (bf16[2,768,768]{2,1,0:T(8,128)(2,1)S(1)}, bf16[2,768,768]{2,1,0:T(8,128)(2,1)}, u32[]{:S(2)}) copy-start(bf16[2,768,768]{2,1,0:T(8,128)(2,1)} %param.23) | copy-start | bytes 7077892
  247.9 3.7 %copy-start.27 = (f32[4,96,192]{1,2,0:T(8,128)S(1)}, f32[4,96,192]{1,2,0:T(8,128)}, u32[]{:S(2)}) copy-start(f32[4,96,192]{1,2,0:T(8,128)} %slice.68) | copy-start | bytes 884740
  (5 other events, 4.0 us)
Sparse Core Ops, SparseCore 0:
  10.2 20.8 all-gather.5
  87.2 19.9 all-gather.7
